TPU v7x, 128 devices: a whole 4x4x4 slice. The times are simulated.
128 devices in a mesh: slab: 16 (over x, y), sec: 8 (over z, core).
Axes of the slice: x: 4, y: 4, z: 4, core: 2. Of those that a mesh axis runs over, the one named last changes fastest.
Arguments:
- coefficients: float32 [17, 12, 147456], P(None, None, ('slab', 'sec')), may hold values from -2.4 to 2.4
- azimuths: float32 [8, 147456], P(None, ('slab', 'sec')), may hold values from -3.140625 to 3.140625
- route_rows: int32 [128, 128, 12], P(('slab', 'sec')), may hold values from 0 to 1152, as said below
- face_points: int32 [128, 128, 64], P(('slab', 'sec')), may hold values from 0 to 12288, as said below
- face_nodes: int32 [128, 128, 64], P(('slab', 'sec')), may hold values from 0 to 9600, as said below
- disp_start: float32 [3, 1228800], P(None, ('slab', 'sec')), may hold values from -6 to 6
- veloc_start: float32 [3, 1228800], P(None, ('slab', 'sec')), may hold values from -6 to 6
- memory_start: float32 [9, 125, 16384], P(None, None, ('slab', 'sec')), may hold values from -6 to 6
- connectivity: int32 [125, 16384], P(None, ('slab', 'sec')), may hold values from 0 to 9599, as said below
- x_shared: int32 [2, 71808], P(None, ('slab', 'sec')), may hold values from 0 to 9599, as said below
- y_shared: int32 [2, 71808], P(None, ('slab', 'sec')), may hold values from 0 to 9599, as said below
- absorbing: int32 [16384], P(('slab', 'sec')), may hold values from 0 to 1, as said below
- damping: float32 [16384], P(('slab', 'sec')), may hold values from 0.5 to 10
- modulus: float32 [16384], P(('slab', 'sec')), may hold values from 0.1 to 0.4
- masses: float32 [1228800], P(('slab', 'sec')), may hold values from 1 to 4
Outputs:
- displacement: float32 [3, 1228800], P(None, ('slab', 'sec'))
- velocity: float32 [3, 1228800], P(None, ('slab', 'sec'))
Inputs may be any that keep to these rules, and one draw needn't show every extreme that they name: `route_rows`: 1152 means an empty slot; each source's list holds each of its rows 0..1151 exactly once; some owner receives 12 rows from every source. `face_points`: 12288 means no point. `face_nodes`: 9600 means no node. `connectivity`: local node numbers of a conforming hexahedral GLL mesh, neighbouring elements sharing their face nodes. `x_shared`: local node numbers; entry k of a partition's row 1 is the same physical node as entry k of the next partition's row 0. `y_shared`: local node numbers; entry k of a partition's row 1 is the same physical node as entry k of the next partition's row 0. `absorbing`: 1 marks a bottom layer of one to three elements under each element column of each partition, and outer side layers of one or two elements whose thickness each partition draws for itself.
All inputs are finite; a program needn't handle non-finite values.
Results may differ from a plain program's by a relative error of at most 0.0001.
Values sent between devices are 32-bit elements; how exact they have to be, the bound alone decides.
A program may use at most 128 MiB of HBM per device.

v0:
```python
import math

import jax
import jax.numpy as jnp
import numpy as np
from jax import lax
from jax.experimental import pallas as pl
from jax.experimental.pallas import tpu as pltpu
from jax.sharding import PartitionSpec as P

F32 = jnp.float32
BF16 = jnp.bfloat16
HIGHEST = lax.Precision.HIGHEST
MESH = pl.DeviceIdType.MESH
DT = 0.1
VMEM_LIMIT = 56 * 2**20


def gll_tables():
    points = np.array([-1.0, -math.sqrt(3.0 / 7.0), 0.0, math.sqrt(3.0 / 7.0), 1.0])
    weights = np.array([0.1, 49.0 / 90.0, 32.0 / 45.0, 49.0 / 90.0, 0.1])
    products = np.array(
        [np.prod([points[r] - points[c] for c in range(5) if c != r]) for r in range(5)]
    )
    derivative = np.zeros((5, 5))
    for r in range(5):
        for c in range(5):
            if r != c:
                derivative[r, c] = products[r] / (products[c] * (points[r] - points[c]))
        derivative[r, r] = -derivative[r].sum()
    cube = weights[:, None, None] * weights[None, :, None] * weights[None, None, :]
    eye = np.eye(5)
    grad = np.zeros((3, 128, 128))
    grad[0, :125, :125] = np.kron(derivative, np.kron(eye, eye))
    grad[1, :125, :125] = np.kron(eye, np.kron(derivative, eye))
    grad[2, :125, :125] = np.kron(eye, np.kron(eye, derivative))
    grad = grad.reshape(384, 128).astype(np.float32)
    cube128 = np.zeros((128, 128), np.float32)
    cube128[:125] = cube.reshape(125, 1)
    return grad, np.ascontiguousarray(grad.T), cube128


def split2(x):
    hi = x.astype(BF16)
    return hi, (x - hi.astype(F32)).astype(BF16)


def halves(low, high):
    return jnp.concatenate([low, high], axis=1)


def lanes_of_rows(ref, start, count):
    return jnp.concatenate([ref[pl.ds(start + q, 1), :] for q in range(count)], axis=1)


def one_hot(low, width):
    iota = lax.broadcasted_iota(jnp.int32, (256, width), 0).astype(F32).astype(BF16)
    return jnp.where(iota == jnp.broadcast_to(low.astype(BF16), (256, width)), 1.0, 0.0).astype(BF16)


def synth_kernel(coef_ref, az_ref, route_ref, out_ref, tr_ref):
    rows = az_ref.shape[1]
    tr_ref[...] = jnp.zeros(tr_ref.shape, BF16)
    for blk in range(rows // 128):
        sl = slice(blk * 128, blk * 128 + 128)
        phi = az_ref[:, sl]
        c1 = jnp.cos(phi)
        s1 = jnp.sin(phi)
        acc = [coef_ref[0, :, sl]] * 8
        cm, sm = c1, s1
        for m in range(1, 9):
            cc = coef_ref[m, :, sl]
            cs = coef_ref[8 + m, :, sl]
            for a in range(8):
                acc[a] = acc[a] + cc * cm[a : a + 1, :] + cs * sm[a : a + 1, :]
            cm, sm = cm * c1 - sm * s1, sm * c1 + cm * s1
        stack = jnp.concatenate([acc[a] for a in (0, 2, 4, 6, 1, 3, 5, 7)], axis=0)
        hi, lo = split2(stack)
        tr_ref[0:96, sl] = hi
        tr_ref[128:224, sl] = lo
    lane = lax.broadcasted_iota(jnp.int32, (128, rows), 1)
    for c in range(12):
        pick = jnp.where(route_ref[:, c : c + 1] == lane, 1.0, 0.0).astype(BF16)
        res = lax.dot_general(
            pick, tr_ref[...], (((1,), (1,)), ((), ())), preferred_element_type=F32
        )
        out_ref[pl.ds(c, 128, stride=16), :] = res[:, :128] + res[:, 128:]


def pick_kernel(got_ref, fp_ref, out_ref, tab_ref, h_ref, lo_ref):
    for c in range(12):
        blk = got_ref[pl.ds(c, 128, stride=16), :].T
        hi, lo = split2(halves(blk[0:48], blk[48:96]))
        tab_ref[c * 48 : c * 48 + 48, 0:256] = hi
        tab_ref[c * 48 : c * 48 + 48, 256:512] = lo
    p = halves(fp_ref[0:64, :], fp_ref[64:128, :])
    pf = p.astype(F32)
    a = ((pf + 0.5) * (1.0 / 1536.0)).astype(jnp.int32)
    n = p - a * 1536
    s = ((n.astype(F32) + 0.5) * (1.0 / 12.0)).astype(jnp.int32)
    c = n - s * 12
    h_ref[...] = jnp.where(p >= 12288, 1000, c * 4 + lax.shift_right_logical(a, 1))
    lo_ref[...] = ((jnp.bitwise_and(a, 1) * 128) + s).astype(F32)
    width = 512
    sub12 = lax.broadcasted_iota(jnp.int32, (48, width), 0) // 12
    lane = lax.broadcasted_iota(jnp.int32, (8, 128), 1)

    def body(g, carry):
        oh = one_hot(lanes_of_rows(lo_ref, 4 * g, 4), width)
        res = jnp.dot(
            tab_ref[...], jnp.concatenate([oh, oh], axis=0), preferred_element_type=F32
        )
        hb = jnp.broadcast_to(lanes_of_rows(h_ref, 4 * g, 4), (48, width)) - sub12
        acc = jnp.zeros((48, width), F32)
        for q in range(12):
            acc = jnp.where(hb == 4 * q, res[48 * q : 48 * q + 48], acc)
        acc = acc[0:24] + acc[24:48]
        acc = acc[0:12] + acc[12:24]
        x = acc[0:8]
        y = jnp.concatenate([acc[8:12], acc[8:12]], axis=0)
        for q in range(4):
            xq = x[:, 128 * q : 128 * q + 128]
            yq = y[:, 128 * q : 128 * q + 128]
            row = (4 * g + q) * 8
            out_ref[pl.ds(pl.multiple_of(row, 8), 8), :] = jnp.where(
                lane < 64, xq, pltpu.roll(yq, 64, 1)
            )
            out_ref[pl.ds(pl.multiple_of(row + 512, 8), 8), :] = jnp.where(
                lane < 64, pltpu.roll(xq, 64, 1), yq
            )
        return carry

    lax.fori_loop(0, 16, body, 0)


X0, X4, Y0, Y4, Z0, Z4 = range(6)


def face_pieces(face):
    if face == X0:
        return [(0, 25, 1, 0)]
    if face == X4:
        return [(100, 25, 1, 0)]
    if face == Y0:
        return [(25 * i, 5, 1, 5 * i) for i in range(5)]
    if face == Y4:
        return [(25 * i + 20, 5, 1, 5 * i) for i in range(5)]
    if face == Z0:
        return [(0, 25, 5, 0)]
    return [(4, 25, 5, 0)]


def rows_at(start, count, stride):
    return pl.ds(start, count, stride=stride) if stride > 1 else pl.ds(start, count)


def take_face(f_ref, face, out_ref):
    for c in range(3):
        for start, count, stride, dst in face_pieces(face):
            out_ref[pl.ds(c * 32 + dst, count), :] = f_ref[rows_at(c * 128 + start, count, stride), :]


def add_face(f_ref, face, vals):
    for c in range(3):
        for start, count, stride, dst in face_pieces(face):
            at = rows_at(c * 128 + start, count, stride)
            f_ref[at, :] = f_ref[at, :] + vals[c * 32 + dst : c * 32 + dst + count, :]


def dot3(x, mat):
    hi = x.astype(BF16)
    rest = x - hi.astype(F32)
    mid, low = split2(rest)
    parts = jnp.concatenate([hi, mid, low], axis=0)
    n = x.shape[0]
    res = jnp.dot(parts, mat, preferred_element_type=F32)
    return res[0:n] + res[n : 2 * n] + res[2 * n : 3 * n]


def column(row):
    return jnp.broadcast_to(row, (128, 128)).T


def match(col, row, good):
    return jnp.where((col == row) & good, 1.0, 0.0).astype(BF16)


def main_kernel(
    n_slab,
    n_sec,
    arr_ref,
    fn_ref,
    disp_ref,
    veloc_ref,
    mem_ref,
    conn_ref,
    xs_ref,
    ys_ref,
    absorb_ref,
    damp_ref,
    mod_ref,
    mass_ref,
    grad_ref,
    gradt_ref,
    cube_ref,
    outd_ref,
    outv_ref,
    conn_s,
    sh_s,
    tab0_s,
    tabm_s,
    tabi_s,
    st_s,
    ie_s,
    m_s,
    dep_s,
    val_s,
    f_s,
    fa_s,
    fb_s,
    w_s,
    acc_s,
    mat_s,
    kown_s,
    kgot_s,
    send_s,
    recv_s,
    ksem_send,
    ksem_recv,
    sem_send,
    sem_recv,
):
    slab = lax.axis_index("slab")
    sec = lax.axis_index("sec")
    nodes = disp_ref.shape[1]
    groups = -(-nodes // 256)
    nxt_x = lax.rem(slab + 1, n_slab)
    prv_x = lax.rem(slab + n_slab - 1, n_slab)
    nxt_y = lax.rem(sec + 1, n_sec)
    prv_y = lax.rem(sec + n_sec - 1, n_sec)
    targets = [(prv_x, sec), (nxt_x, sec), (slab, prv_y), (slab, nxt_y)]

    barrier = pltpu.get_barrier_semaphore()
    for dev in targets:
        pl.semaphore_signal(barrier, inc=1, device_id=dev, device_id_type=MESH)

    conn_s[...] = jnp.full(conn_s.shape, 1 << 20, jnp.int32)
    conn_s[0:125, :] = conn_ref[...]
    sh_s[...] = jnp.full(sh_s.shape, -1, jnp.int32)
    sh_s[0:2, 0 : xs_ref.shape[1]] = xs_ref[...]
    sh_s[2:4, 0 : ys_ref.shape[1]] = ys_ref[...]

    kown_s[...] = jnp.zeros(kown_s.shape, F32)
    for r, point in ((0, 12), (1, 112), (2, 52), (3, 72)):
        centre = conn_s[point : point + 1, :]
        best = jnp.zeros((128, 128), jnp.int32)
        for b in range(5):
            col = column(sh_s[r : r + 1, b * 128 : b * 128 + 128])
            slot = lax.broadcasted_iota(jnp.int32, (128, 128), 0) + (b * 128 + 1)
            best = jnp.maximum(best, jnp.where(col == centre, slot, 0))
        kown_s[r : r + 1, :] = jnp.max(best, axis=0, keepdims=True).astype(F32)

    pl.semaphore_wait(barrier, 4)
    kcopies = []
    for d, dev in enumerate(targets):
        copy = pltpu.make_async_remote_copy(
            src_ref=kown_s,
            dst_ref=kgot_s.at[d ^ 1],
            send_sem=ksem_send.at[d],
            recv_sem=ksem_recv.at[d ^ 1],
            device_id=dev,
            device_id_type=MESH,
        )
        copy.start()
        kcopies.append(copy)

    tab0_s[...] = jnp.zeros(tab0_s.shape, F32)
    tab0_s[0:3, 0:nodes] = disp_ref[...]
    tab0_s[3:6, 0:nodes] = veloc_ref[...]
    tab0_s[6:7, 0:nodes] = mass_ref[...]
    for h2 in range(groups // 2):
        two = jnp.concatenate(
            [tab0_s[:, h2 * 512 : h2 * 512 + 256], tab0_s[:, h2 * 512 + 256 : h2 * 512 + 512]], axis=0
        )
        hi, lo = split2(two)
        tabm_s[h2 * 16 : h2 * 16 + 16, 0:256] = hi
        tabm_s[h2 * 16 : h2 * 16 + 16, 256:512] = lo

    width = 512

    def pick_state(g, carry):
        idx = lanes_of_rows(conn_s, 4 * g, 4)
        oh = one_hot(jnp.bitwise_and(idx, 255).astype(F32), width)
        res = jnp.dot(
            tabm_s[...], jnp.concatenate([oh, oh], axis=0), preferred_element_type=F32
        )
        hb = jnp.broadcast_to(lax.shift_right_logical(idx, 8), (8, width))
        acc = jnp.zeros((8, width), F32)
        for h in range(groups):
            acc = jnp.where(hb == h, res[8 * h : 8 * h + 8], acc)
        for q in range(4):
            st_s[pl.ds(4 * g + q, 8, stride=128), :] = acc[:, 128 * q : 128 * q + 128]
        return carry

    lax.fori_loop(0, 32, pick_state, 0)

    sub12 = lax.broadcasted_iota(jnp.int32, (48, 256), 0) // 12
    lane = lax.broadcasted_iota(jnp.int32, (8, 128), 1)
    dep_s[...] = jnp.zeros(dep_s.shape, F32)

    def deposit(g, carry):
        vals = []
        idxs = []
        for q in range(2):
            row = (2 * g + q) * 8
            c0 = arr_ref[pl.ds(pl.multiple_of(row, 8), 8), :]
            c1 = arr_ref[pl.ds(pl.multiple_of(row + 512, 8), 8), :]
            x = jnp.where(lane < 64, c0, pltpu.roll(c1, 64, 1))
            y = jnp.where(lane < 64, pltpu.roll(c0, 64, 1), c1)
            v12 = jnp.concatenate([x, y[0:4]], axis=0)
            v24 = jnp.concatenate([v12, v12], axis=0)
            vals.append(jnp.concatenate([v24, v24], axis=0))
            idxs.append(halves(fn_ref[pl.ds(2 * g + q, 1), :], fn_ref[pl.ds(2 * g + q + 64, 1), :]))
        val = jnp.concatenate(vals, axis=1)
        idx = jnp.concatenate(idxs, axis=1)
        idx = jnp.where(idx >= nodes, 1 << 20, idx)
        vhi, vlo = split2(val)
        oh = one_hot(jnp.bitwise_and(idx, 255).astype(F32), 256)
        high = jnp.minimum(lax.shift_right_logical(idx, 8), 200)
        hb = (jnp.broadcast_to(high, (48, 256)) - sub12).astype(F32).astype(BF16)
        zero = jnp.zeros((48, 256), BF16)
        lhs = []
        for q in range(10):
            mask = hb == jnp.asarray(4 * q, BF16)
            lhs.append(halves(jnp.where(mask, vhi, zero), jnp.where(mask, vlo, zero)))
        lhs = jnp.concatenate(lhs, axis=0)
        dep_s[...] += lax.dot_general(
            lhs, halves(oh, oh), (((1,), (1,)), ((), ())), preferred_element_type=F32
        )
        return carry

    lax.fori_loop(0, 32, deposit, 0)

    hi, lo = split2(dep_s[...])
    tabi_s[:, 0:256] = hi
    tabi_s[:, 256:512] = lo
    sub12w = lax.broadcasted_iota(jnp.int32, (48, width), 0) // 12

    def pick_inj(g, carry):
        idx = lanes_of_rows(conn_s, 4 * g, 4)
        oh = one_hot(jnp.bitwise_and(idx, 255).astype(F32), width)
        res = jnp.dot(
            tabi_s[...], jnp.concatenate([oh, oh], axis=0), preferred_element_type=F32
        )
        hb = jnp.broadcast_to(lax.shift_right_logical(idx, 8), (48, width)) - sub12w
        acc = jnp.zeros((48, width), F32)
        for q in range(10):
            acc = jnp.where(hb == 4 * q, res[48 * q : 48 * q + 48], acc)
        acc = acc[0:24] + acc[24:48]
        acc = acc[0:12] + acc[12:24]
        for q in range(4):
            part = acc[:, 128 * q : 128 * q + 128]
            ie_s[pl.ds(4 * g + q, 8, stride=128), :] = part[0:8]
            ie_s[pl.ds(8 * 128 + 4 * g + q, 4, stride=128), :] = part[8:12]
        return carry

    lax.fori_loop(0, 32, pick_inj, 0)

    for copy in kcopies:
        copy.wait()
    true = jnp.full((128, 128), True)
    for d, (low_point, high_point) in enumerate(((12, 112), (52, 72), (60, 64))):
        low = conn_s[low_point : low_point + 1, :]
        high = conn_s[high_point : high_point + 1, :]
        mat_s[2 * d, 0:128, :] = match(column(high), low, true)
        mat_s[2 * d + 1, 0:128, :] = match(column(low), high, true)
        if d < 2:
            pos, count = ((slab, n_slab), (sec, n_sec))[d]
            low_k = kown_s[2 * d : 2 * d + 1, :]
            high_k = kown_s[2 * d + 1 : 2 * d + 2, :]
            from_prev = column(kgot_s[2 * d, 2 * d + 1 : 2 * d + 2, :])
            from_next = column(kgot_s[2 * d + 1, 2 * d : 2 * d + 1, :])
            mat_s[2 * d, 128:256, :] = match(from_prev, low_k, (low_k > 0.5) & (pos > 0))
            mat_s[2 * d + 1, 128:256, :] = match(
                from_next, high_k, (high_k > 0.5) & (pos < count - 1)
            )

    def local_sum(d):
        take_face(f_s, 2 * d, fa_s)
        take_face(f_s, 2 * d + 1, fb_s)
        into_low = dot3(fb_s[...], mat_s[2 * d, 0:128, :])
        into_high = dot3(fa_s[...], mat_s[2 * d + 1, 0:128, :])
        add_face(f_s, 2 * d, into_low)
        add_face(f_s, 2 * d + 1, into_high)

    fa_s[...] = jnp.zeros(fa_s.shape, F32)
    fb_s[...] = jnp.zeros(fb_s.shape, F32)
    send_s[...] = jnp.zeros(send_s.shape, F32)
    f_s[...] = jnp.ones(f_s.shape, F32)
    for d in range(3):
        local_sum(d)
    w_s[...] = 1.0 / f_s[0:128, :]

    absorb = absorb_ref[...].astype(F32)
    retain = jnp.exp(-DT * damp_ref[...])
    m_s[...] = jnp.zeros(m_s.shape, F32)
    for d in range(3):
        for c in range(3):
            m_s[d * 128 : d * 128 + 125, c * 128 : c * 128 + 128] = mem_ref[3 * d + c]
    row = lax.broadcasted_iota(jnp.int32, (128, 128), 0)
    mass = st_s[768:896, :]
    st_s[896:1024, :] = jnp.where(row < 125, DT / jnp.where(row < 125, mass, 1.0), 0.0)
    acc_s[...] = jnp.zeros(acc_s.shape, F32)

    def step(n, carry):
        u = jnp.concatenate([st_s[c * 128 : c * 128 + 128, :] for c in range(3)], axis=1)
        g = jnp.dot(grad_ref[...], u, precision=HIGHEST, preferred_element_type=F32)
        wide = lambda x: jnp.concatenate([x, x, x], axis=1)
        ab, rt = wide(absorb), wide(retain)
        weight = wide(mod_ref[...] * cube_ref[...])
        weight = jnp.concatenate([weight, weight, weight], axis=0)
        mem = m_s[...]
        stress = weight * (g - ab * mem)
        m_s[...] = ab * (rt * mem + (1.0 - rt) * g)
        div = jnp.dot(gradt_ref[...], stress, precision=HIGHEST, preferred_element_type=F32)
        for c in range(3):
            at = slice(c * 128, c * 128 + 128)
            inj = ie_s[pl.ds(pl.multiple_of(n * 384 + c * 128, 128), 128), :]
            f_s[at, :] = w_s[...] * inj - div[:, at]
        for d in range(2):
            sends = []
            for side in range(2):
                part = 2 * d + side
                take_face(f_s, part, send_s.at[part])
            for side in range(2):
                part = 2 * d + side
                copy = pltpu.make_async_remote_copy(
                    src_ref=send_s.at[part],
                    dst_ref=recv_s.at[n, part ^ 1],
                    send_sem=sem_send.at[n, part],
                    recv_sem=sem_recv.at[n, part ^ 1],
                    device_id=targets[part],
                    device_id_type=MESH,
                )
                copy.start()
                sends.append(copy)
            into_low = dot3(send_s[2 * d + 1], mat_s[2 * d, 0:128, :])
            into_high = dot3(send_s[2 * d], mat_s[2 * d + 1, 0:128, :])
            for copy in sends:
                copy.wait()
            into_low += dot3(recv_s[n, 2 * d], mat_s[2 * d, 128:256, :])
            into_high += dot3(recv_s[n, 2 * d + 1], mat_s[2 * d + 1, 128:256, :])
            add_face(f_s, 2 * d, into_low)
            add_face(f_s, 2 * d + 1, into_high)
        local_sum(2)
        total = f_s[...]
        scale = st_s[896:1024, :]
        scale = jnp.concatenate([scale, scale, scale], axis=0)
        v = st_s[384:768, :] + total * scale
        st_s[384:768, :] = v
        st_s[0:384, :] = st_s[0:384, :] + DT * v
        w3 = jnp.concatenate([w_s[...], w_s[...], w_s[...]], axis=0)
        own = w3 * (total - ie_s[pl.ds(pl.multiple_of(n * 384, 128), 384), :])
        acc_s[0:384, :] = acc_s[0:384, :] + own
        acc_s[384:768, :] = acc_s[384:768, :] + (4 - n).astype(F32) * own
        return carry

    lax.fori_loop(0, 4, step, 0)

    val_s[...] = jnp.zeros(val_s.shape, F32)
    sub8 = lax.broadcasted_iota(jnp.int32, (16, width), 0) // 8

    def collect(g, carry):
        idx = lanes_of_rows(conn_s, 4 * g, 4)
        vals = []
        for q in range(4):
            six = acc_s[pl.ds(4 * g + q, 8, stride=128), :]
            vals.append(jnp.concatenate([six, six], axis=0))
        vhi, vlo = split2(jnp.concatenate(vals, axis=1))
        oh = one_hot(jnp.bitwise_and(idx, 255).astype(F32), width)
        high = jnp.minimum(lax.shift_right_logical(idx, 8), 200)
        hb = (jnp.broadcast_to(high, (16, width)) - sub8).astype(F32).astype(BF16)
        zero = jnp.zeros((16, width), BF16)
        lhs = []
        for q in range(groups // 2):
            mask = hb == jnp.asarray(2 * q, BF16)
            lhs.append(halves(jnp.where(mask, vhi, zero), jnp.where(mask, vlo, zero)))
        lhs = jnp.concatenate(lhs, axis=0)
        val_s[...] += lax.dot_general(
            lhs, halves(oh, oh), (((1,), (1,)), ((), ())), preferred_element_type=F32
        )
        return carry

    lax.fori_loop(0, 32, collect, 0)

    for h in range(groups):
        size = min(256, nodes - h * 256)
        at = slice(h * 256, h * 256 + size)
        lanes = slice(0, size)
        inv = DT / mass_ref[:, at]
        inj = [dep_s[12 * h + 3 * n : 12 * h + 3 * n + 3, lanes] for n in range(4)]
        vsum = inj[0] + inj[1] + inj[2] + inj[3] + val_s[8 * h : 8 * h + 3, lanes]
        usum = 4.0 * inj[0] + 3.0 * inj[1] + 2.0 * inj[2] + inj[3] + val_s[8 * h + 3 : 8 * h + 6, lanes]
        v0 = veloc_ref[:, at]
        outv_ref[:, at] = v0 + inv * vsum
        outd_ref[:, at] = disp_ref[:, at] + (4.0 * DT) * v0 + (DT * inv) * usum


def local(n_slab, n_sec):
    grad, gradt, cube = gll_tables()
    params = pltpu.CompilerParams(vmem_limit_bytes=VMEM_LIMIT)
    vmem = pl.BlockSpec(memory_space=pltpu.VMEM)

    def run(
        coefficients,
        azimuths,
        route_rows,
        face_points,
        face_nodes,
        disp_start,
        veloc_start,
        memory_start,
        connectivity,
        x_shared,
        y_shared,
        absorbing,
        damping,
        modulus,
        masses,
    ):
        devices = n_slab * n_sec
        rows = azimuths.shape[1]
        nodes = disp_start.shape[1]
        payload = pl.pallas_call(
            synth_kernel,
            out_shape=jax.ShapeDtypeStruct((devices * 16, 128), F32),
            in_specs=[vmem] * 3,
            out_specs=vmem,
            scratch_shapes=[pltpu.VMEM((256, rows), BF16)],
            compiler_params=params,
            name="synthesis",
        )(coefficients, azimuths, route_rows.reshape(devices, 12))
        got = lax.all_to_all(
            payload.reshape(devices, 16, 128), ("slab", "sec"), split_axis=0, concat_axis=0, tiled=True
        )
        sent = pl.pallas_call(
            pick_kernel,
            out_shape=jax.ShapeDtypeStruct((devices * 8, 128), F32),
            in_specs=[vmem] * 2,
            out_specs=vmem,
            scratch_shapes=[
                pltpu.VMEM((576, 512), BF16),
                pltpu.VMEM((64, 128), jnp.int32),
                pltpu.VMEM((64, 128), F32),
            ],
            compiler_params=params,
            name="points",
        )(got.reshape(devices * 16, 128), face_points.reshape(devices, 64))
        arrived = lax.all_to_all(
            sent.reshape(devices, 8, 128), ("slab", "sec"), split_axis=0, concat_axis=0, tiled=True
        )
        groups = -(-nodes // 256)
        dma = pltpu.SemaphoreType.DMA
        return pl.pallas_call(
            lambda *refs: main_kernel(n_slab, n_sec, *refs),
            out_shape=(
                jax.ShapeDtypeStruct((3, nodes), F32),
                jax.ShapeDtypeStruct((3, nodes), F32),
            ),
            in_specs=[vmem] * 15,
            out_specs=(vmem, vmem),
            scratch_shapes=[
                pltpu.VMEM((128, 128), jnp.int32),
                pltpu.VMEM((8, 640), jnp.int32),
                pltpu.VMEM((8, groups * 256), F32),
                pltpu.VMEM((groups * 8, 512), BF16),
                pltpu.VMEM((480, 512), BF16),
                pltpu.VMEM((1024, 128), F32),
                pltpu.VMEM((1536, 128), F32),
                pltpu.VMEM((384, 384), F32),
                pltpu.VMEM((480, 256), F32),
                pltpu.VMEM((groups * 8, 256), F32),
                pltpu.VMEM((384, 128), F32),
                pltpu.VMEM((96, 128), F32),
                pltpu.VMEM((96, 128), F32),
                pltpu.VMEM((128, 128), F32),
                pltpu.VMEM((1024, 128), F32),
                pltpu.VMEM((6, 256, 128), BF16),
                pltpu.VMEM((8, 128), F32),
                pltpu.VMEM((4, 8, 128), F32),
                pltpu.VMEM((4, 96, 128), F32),
                pltpu.VMEM((4, 4, 96, 128), F32),
                dma((4,)),
                dma((4,)),
                dma((4, 4)),
                dma((4, 4)),
            ],
            compiler_params=pltpu.CompilerParams(
                vmem_limit_bytes=VMEM_LIMIT, collective_id=0, has_side_effects=True
            ),
            name="slab_steps",
        )(
            arrived.reshape(devices * 8, 128),
            face_nodes.reshape(devices, 64),
            disp_start,
            veloc_start,
            memory_start,
            connectivity,
            x_shared,
            y_shared,
            absorbing.reshape(1, -1),
            damping.reshape(1, -1),
            modulus.reshape(1, -1),
            masses.reshape(1, -1),
            grad,
            gradt,
            cube,
        )

    return run


def solution(mesh):
    both = ("slab", "sec")
    return jax.shard_map(
        local(mesh.shape["slab"], mesh.shape["sec"]),
        mesh=mesh,
        in_specs=(
            P(None, None, both),
            P(None, both),
            P(both, None, None),
            P(both, None, None),
            P(both, None, None),
            P(None, both),
            P(None, both),
            P(None, None, both),
            P(None, both),
            P(None, both),
            P(None, both),
            P(both),
            P(both),
            P(both),
            P(both),
        ),
        out_specs=(P(None, both), P(None, both)),
        check_vma=False,
    )
```

profile of v0, /device:TPU:1, one launch (start us, length us, event | category | flops | bytes accessed | tf_op | source)
XLA Modules:
  0.0 173.4 jit_solution(6524672985679166042)
XLA Ops:
  0.6 1.4 copy.20
  2.1 5.7 %synthesis.1 = f32[2048,128]{1,0:T(8,128)} custom-call(f32[17,12,1152]{2,1,0:T(8,128)} %coef_ref.1, f32[8,1152]{1,0:T(8,128)} %az_ref.1, s32[128,12]{1,0:T(8,128)} %bitcast.16), custom_call_target="tpu_custom_call" | custom-call | tf_op jit(solution)/shard_map/synthesis/pallas_call | solution.py:534
  7.8 0.0 copy-start.3
  7.8 11.5 %all-to-all-start = ((f32[128,16,128]{2,1,0:T(8,128)}), f32[128,16,128]{2,1,0:T(8,128)S(1)}, u32[]{:S(2)}, u32[]{:S(2)}) async-start(f32[128,16,128]{2,1,0:T(8,128)} %bitcast.10), calls=%async_computation | async-start | bytes 2097152 | tf_op jit(solution)/shard_map/all_to_all | solution.py:543
  19.3 0.0 copy-done.3
  19.3 0.7 copy.21
  20.0 18.5 %all-to-all-done = f32[128,16,128]{2,1,0:T(8,128)S(1)} async-done(((f32[128,16,128]{2,1,0:T(8,128)}), f32[128,16,128]{2,1,0:T(8,128)S(1)}, u32[]{:S(2)}, u32[]{:S(2)}) %all-to-all-start) | async-done | bytes 1048608 | tf_op jit(solution)/shard_map/all_to_all | solution.py:543
  38.6 0.0 copy-start
  38.6 1.0 copy-done
  39.5 0.0 copy-start.4
  39.5 0.0 copy-start.2
  39.5 12.6 %points.1 = f32[1024,128]{1,0:T(8,128)} custom-call(f32[2048,128]{1,0:T(8,128)} %bitcast.11, s32[128,64]{1,0:T(8,128)} %bitcast.15), custom_call_target="tpu_custom_call" | custom-call | tf_op jit(solution)/shard_map/points/pallas_call | solution.py:546
  52.2 4.6 %all-to-all-start.1 = ((f32[128,8,128]{2,1,0:T(8,128)}), f32[128,8,128]{2,1,0:T(8,128)S(1)}, u32[]{:S(2)}, u32[]{:S(2)}) async-start(f32[128,8,128]{2,1,0:T(8,128)} %bitcast.13), calls=%async_computation.1 | async-start | bytes 1048576 | tf_op jit(solution)/shard_map/all_to_all | solution.py:559
  56.8 0.0 copy-done.4
  56.8 0.7 copy.22
  57.5 0.0 copy-done.2
  57.5 0.6 reshape.47.refs_11_
  58.2 12.4 %all-to-all-done.1 = f32[128,8,128]{2,1,0:T(8,128)S(1)} async-done(((f32[128,8,128]{2,1,0:T(8,128)}), f32[128,8,128]{2,1,0:T(8,128)S(1)}, u32[]{:S(2)}, u32[]{:S(2)}) %all-to-all-start.1) | async-done | bytes 524320 | tf_op jit(solution)/shard_map/all_to_all | solution.py:559
  70.6 0.0 copy-start.1
  70.6 0.8 copy-done.1
  71.4 98.8 %slab_steps.1 = (f32[3,9600]{1,0:T(4,128)}, f32[3,9600]{1,0:T(4,128)}) custom-call(f32[1024,128]{1,0:T(8,128)} %bitcast.12, s32[128,64]{1,0:T(8,128)} %bitcast.14, f32[3,9600]{1,0:T(4,128)} %refs_2_.1, f32[3,9600]{1,0:T(4,128)} %refs_3_.1, f32[9,125,128]{2,1,0:T(8,128)} %refs_4_.1, s32[125,128]{1,0:T(8,128)} %refs_5_.1, s32[2,561]{1,0:T(2,128)} %refs_6_.1, ...), custom_call_target="tpu_custom_call" | custom-call | tf_op jit(solution)/shard_map/slab_steps/pallas_call | solution.py:564
  170.2 1.6 copy.25
  171.8 1.6 copy.26
Async XLA Ops:
  7.8 11.5 %copy-start.3 = (s32[1,128,64]{1,2,0:T(8,128)S(1)}, s32[1,128,64]{1,2,0:T(8,128)}, u32[]{:S(2)}) copy-start(s32[1,128,64]{1,2,0:T(8,128)} %param.21) | copy-start | bytes 98308
  7.8 30.8 %all-to-all-start = ((f32[128,16,128]{2,1,0:T(8,128)}), f32[128,16,128]{2,1,0:T(8,128)S(1)}, u32[]{:S(2)}, u32[]{:S(2)}) async-start(f32[128,16,128]{2,1,0:T(8,128)} %bitcast.10), calls=%async_computation | async-start | bytes 2097152 | tf_op jit(solution)/shard_map/all_to_all | solution.py:543
  38.6 1.0 copy-start
  39.5 17.3 %copy-start.4 = (s32[1,128,64]{1,2,0:T(8,128)S(1)}, s32[1,128,64]{1,2,0:T(8,128)}, u32[]{:S(2)}) copy-start(s32[1,128,64]{1,2,0:T(8,128)} %param.22) | copy-start | bytes 98308
  39.5 18.0 %copy-start.2 = (f32[9600]{0:T(1024)S(1)}, f32[9600]{0:T(1024)}, u32[]{:S(2)}) copy-start(f32[9600]{0:T(1024)} %param.32) | copy-start | bytes 115204
  52.2 18.4 %all-to-all-start.1 = ((f32[128,8,128]{2,1,0:T(8,128)}), f32[128,8,128]{2,1,0:T(8,128)S(1)}, u32[]{:S(2)}, u32[]{:S(2)}) async-start(f32[128,8,128]{2,1,0:T(8,128)} %bitcast.13), calls=%async_computation.1 | async-start | bytes 1048576 | tf_op jit(solution)/shard_map/all_to_all | solution.py:559
  70.6 0.8 copy-start.1
where the time goes:
time: 174 us; the launch traced here: 173 us
  Pallas kernels  117 us (67%)
  waiting for transfers between devices  31 us (18%)
  starting transfers between devices  16.1 us (9%)
  local copies, waits for them, and re-layouts  8.5 us (5%)
    pallas_call x1, Pallas kernels, run(): pl.pallas_call(lambda *refs: main_kernel(n_slab, n_sec, *refs), out_shape...  98.8 us
    all_to_all x1, waiting for transfers between devices, run(): lax.all_to_all(payload.reshape(devices, 16, 128), ('slab', 'sec'), split_...  18.5 us
    pallas_call x1, Pallas kernels, run(): pl.pallas_call(pick_kernel, out_shape=jax.ShapeDtypeStruct((devices * 8,...  12.6 us
    all_to_all x1, waiting for transfers between devices, run(): lax.all_to_all(sent.reshape(devices, 8, 128), ('slab', 'sec'), split_axis...  12.4 us
    all_to_all x1, starting transfers between devices, run(): lax.all_to_all(payload.reshape(devices, 16, 128), ('slab', 'sec'), split_...  11.5 us
    unnamed x15, local copies, waits for them, and re-layouts  7.86 us
    pallas_call x1, Pallas kernels, run(): pl.pallas_call(synth_kernel, out_shape=jax.ShapeDtypeStruct((devices * 16...  5.74 us
    all_to_all x1, starting transfers between devices, run(): lax.all_to_all(sent.reshape(devices, 8, 128), ('slab', 'sec'), split_axis...  4.62 us
  transfers between devices with their start and end apart: 2, of which 2 were waited for; matrix products, arithmetic and copies ran while one was open for 1% of the time, Pallas kernels for 0%

commit v1 on v0

v1 whole, which is shorter than its diff:
```python
import math

import jax
import jax.numpy as jnp
import numpy as np
from jax import lax
from jax.experimental import pallas as pl
from jax.experimental.pallas import tpu as pltpu
from jax.sharding import PartitionSpec as P

F32 = jnp.float32
BF16 = jnp.bfloat16
HIGHEST = lax.Precision.HIGHEST
MESH = pl.DeviceIdType.MESH
DT = 0.1
VMEM_LIMIT = 56 * 2**20


def gll_tables():
    points = np.array([-1.0, -math.sqrt(3.0 / 7.0), 0.0, math.sqrt(3.0 / 7.0), 1.0])
    weights = np.array([0.1, 49.0 / 90.0, 32.0 / 45.0, 49.0 / 90.0, 0.1])
    products = np.array(
        [np.prod([points[r] - points[c] for c in range(5) if c != r]) for r in range(5)]
    )
    derivative = np.zeros((5, 5))
    for r in range(5):
        for c in range(5):
            if r != c:
                derivative[r, c] = products[r] / (products[c] * (points[r] - points[c]))
        derivative[r, r] = -derivative[r].sum()
    cube = weights[:, None, None] * weights[None, :, None] * weights[None, None, :]
    eye = np.eye(5)
    grad = np.zeros((3, 128, 128))
    grad[0, :125, :125] = np.kron(derivative, np.kron(eye, eye))
    grad[1, :125, :125] = np.kron(eye, np.kron(derivative, eye))
    grad[2, :125, :125] = np.kron(eye, np.kron(eye, derivative))
    grad = grad.reshape(384, 128).astype(np.float32)
    cube128 = np.zeros((128, 128), np.float32)
    cube128[:125] = cube.reshape(125, 1)
    return grad, np.ascontiguousarray(grad.T), cube128


def split2(x):
    hi = x.astype(BF16)
    return hi, (x - hi.astype(F32)).astype(BF16)


def halves(low, high):
    return jnp.concatenate([low, high], axis=1)


def lanes_of_rows(ref, start, count):
    return jnp.concatenate([ref[pl.ds(start + q, 1), :] for q in range(count)], axis=1)


def one_hot(low, width):
    iota = lax.broadcasted_iota(jnp.int32, (256, width), 0).astype(F32).astype(BF16)
    hit = iota == jnp.broadcast_to(low.astype(F32).astype(BF16), (256, width))
    return jnp.where(hit, jnp.ones((256, width), BF16), jnp.zeros((256, width), BF16))


X0, X4, Y0, Y4, Z0, Z4 = range(6)


def face_pieces(face):
    if face == X0:
        return [(0, 25, 1, 0)]
    if face == X4:
        return [(100, 25, 1, 0)]
    if face == Y0:
        return [(25 * i, 5, 1, 5 * i) for i in range(5)]
    if face == Y4:
        return [(25 * i + 20, 5, 1, 5 * i) for i in range(5)]
    if face == Z0:
        return [(0, 25, 5, 0)]
    return [(4, 25, 5, 0)]


def rows_at(start, count, stride):
    return pl.ds(start, count, stride=stride) if stride > 1 else pl.ds(start, count)


def take_face(f_ref, face, out_ref):
    for c in range(3):
        for start, count, stride, dst in face_pieces(face):
            out_ref[pl.ds(c * 32 + dst, count), :] = f_ref[rows_at(c * 128 + start, count, stride), :]


def add_face(f_ref, face, vals):
    for c in range(3):
        for start, count, stride, dst in face_pieces(face):
            at = rows_at(c * 128 + start, count, stride)
            f_ref[at, :] = f_ref[at, :] + vals[c * 32 + dst : c * 32 + dst + count, :]


def dot3(x, mat):
    hi = x.astype(BF16)
    rest = x - hi.astype(F32)
    mid, low = split2(rest)
    parts = jnp.concatenate([hi, mid, low], axis=0)
    n = x.shape[0]
    res = jnp.dot(parts, mat, preferred_element_type=F32)
    return res[0:n] + res[n : 2 * n] + res[2 * n : 3 * n]


def column(row):
    return jnp.broadcast_to(row, (128, 128)).T


def match(col, row, good):
    return jnp.where((col == row) & good, 1.0, 0.0).astype(BF16)


def synthesize(coef_ref, az_ref, route_ref, tr_ref, send_ref):
    rows = az_ref.shape[1]
    tr_ref[...] = jnp.zeros(tr_ref.shape, BF16)
    for blk in range(rows // 128):
        sl = slice(blk * 128, blk * 128 + 128)
        phi = az_ref[:, sl]
        c1 = jnp.cos(phi)
        s1 = jnp.sin(phi)
        acc = [coef_ref[0, :, sl]] * 8
        cm, sm = c1, s1
        for m in range(1, 9):
            cc = coef_ref[m, :, sl]
            cs = coef_ref[8 + m, :, sl]
            for a in range(8):
                acc[a] = acc[a] + cc * cm[a : a + 1, :] + cs * sm[a : a + 1, :]
            cm, sm = cm * c1 - sm * s1, sm * c1 + cm * s1
        stack = jnp.concatenate([acc[a] for a in (0, 2, 4, 6, 1, 3, 5, 7)], axis=0)
        hi, lo = split2(stack)
        tr_ref[0:96, sl] = hi
        tr_ref[128:224, sl] = lo
    lane = lax.broadcasted_iota(jnp.int32, (128, rows), 1)
    lane1 = lax.broadcasted_iota(jnp.int32, (128, 128), 1)
    for quad in range(3):
        got = []
        for c in range(4 * quad, 4 * quad + 4):
            col = jnp.concatenate([column(route_ref[c])] * (rows // 128), axis=1)
            pick = jnp.where(col == lane, 1.0, 0.0).astype(BF16)
            res = lax.dot_general(
                pick, tr_ref[...], (((1,), (1,)), ((), ())), preferred_element_type=F32
            )
            got.append(res[:, :128] + res[:, 128:])
        b1 = pltpu.roll(got[1], 96, 1)
        b2 = pltpu.roll(got[2], 64, 1)
        b3 = pltpu.roll(got[3], 32, 1)
        send_ref[pl.ds(3 * quad, 128, stride=16), :] = jnp.where(lane1 < 96, got[0], b1)
        send_ref[pl.ds(3 * quad + 1, 128, stride=16), :] = jnp.where(lane1 < 64, b1, b2)
        send_ref[pl.ds(3 * quad + 2, 128, stride=16), :] = jnp.where(lane1 < 32, b2, b3)


def paired(ref):
    two = jnp.concatenate([ref[...], ref[...]], axis=0).T
    lane = lax.broadcasted_iota(jnp.int32, (64, 128), 1)
    return jnp.where(lane < 64, two[0:64], two[64:128])


def mega_kernel(
    n_slab,
    n_sec,
    coef_ref,
    az_ref,
    route_ref,
    fp_ref,
    fn_ref,
    disp_ref,
    veloc_ref,
    mem_ref,
    conn_ref,
    xs_ref,
    ys_ref,
    absorb_ref,
    damp_ref,
    mod_ref,
    mass_ref,
    grad_ref,
    gradt_ref,
    cube_ref,
    outd_ref,
    outv_ref,
    tr_s,
    rows_send,
    rows_got,
    pts_send,
    pts_got,
    tabp_s,
    h_s,
    lo_s,
    fn_s,
    conn_s,
    sh_s,
    tab0_s,
    tabm_s,
    tabi_s,
    st_s,
    ie_s,
    m_s,
    dep_s,
    val_s,
    f_s,
    fa_s,
    fb_s,
    w_s,
    acc_s,
    mat_s,
    kown_s,
    kgot_s,
    send_s,
    recv_s,
    ksem_send,
    ksem_recv,
    sem_send,
    sem_recv,
    rsem_send,
    rsem_recv,
    psem_send,
    psem_recv,
):
    slab = lax.axis_index("slab")
    sec = lax.axis_index("sec")
    me = slab * n_sec + sec
    devices = n_slab * n_sec
    nodes = disp_ref.shape[1]
    groups = -(-nodes // 256)
    nxt_x = lax.rem(slab + 1, n_slab)
    prv_x = lax.rem(slab + n_slab - 1, n_slab)
    nxt_y = lax.rem(sec + 1, n_sec)
    prv_y = lax.rem(sec + n_sec - 1, n_sec)
    targets = [(prv_x, sec), (nxt_x, sec), (slab, prv_y), (slab, nxt_y)]

    def place(d):
        return (d // n_sec, lax.rem(d, n_sec))

    barrier = pltpu.get_barrier_semaphore()

    def greet(j, carry):
        d = lax.rem(me + j, devices)
        pl.semaphore_signal(barrier, inc=1, device_id=place(d), device_id_type=MESH)
        return carry

    lax.fori_loop(1, devices, greet, 0)

    synthesize(coef_ref, az_ref, route_ref, tr_s, rows_send)

    pl.semaphore_wait(barrier, devices - 1)

    def send_rows(j, carry):
        d = lax.rem(me + j, devices)
        pltpu.make_async_remote_copy(
            src_ref=rows_send.at[pl.ds(d * 16, 9)],
            dst_ref=rows_got.at[pl.ds(me * 16, 9)],
            send_sem=rsem_send,
            recv_sem=rsem_recv,
            device_id=place(d),
            device_id_type=MESH,
        ).start()
        return carry

    lax.fori_loop(1, devices, send_rows, 0)
    own = pl.ds(pl.multiple_of(me * 16, 16), 16)
    rows_got[own, :] = rows_send[own, :]

    conn_s[...] = jnp.full(conn_s.shape, 1 << 20, jnp.int32)
    conn_s[0:125, :] = conn_ref[...]
    sh_s[...] = jnp.full(sh_s.shape, -1, jnp.int32)
    sh_s[0:2, 0 : xs_ref.shape[1]] = xs_ref[...]
    sh_s[2:4, 0 : ys_ref.shape[1]] = ys_ref[...]

    kown_s[...] = jnp.zeros(kown_s.shape, F32)
    for r, point in ((0, 12), (1, 112), (2, 52), (3, 72)):
        centre = conn_s[point : point + 1, :]
        best = jnp.zeros((128, 128), jnp.int32)
        for b in range(5):
            col = column(sh_s[r : r + 1, b * 128 : b * 128 + 128])
            slot = lax.broadcasted_iota(jnp.int32, (128, 128), 0) + (b * 128 + 1)
            best = jnp.maximum(best, jnp.where(col == centre, slot, 0))
        kown_s[r : r + 1, :] = jnp.max(best, axis=0, keepdims=True).astype(F32)
    kcopies = []
    for d, dev in enumerate(targets):
        copy = pltpu.make_async_remote_copy(
            src_ref=kown_s,
            dst_ref=kgot_s.at[d ^ 1],
            send_sem=ksem_send.at[d],
            recv_sem=ksem_recv.at[d ^ 1],
            device_id=dev,
            device_id_type=MESH,
        )
        copy.start()
        kcopies.append(copy)

    tab0_s[...] = jnp.zeros(tab0_s.shape, F32)
    tab0_s[0:3, 0:nodes] = disp_ref[...]
    tab0_s[3:6, 0:nodes] = veloc_ref[...]
    for h in range(nodes // 128):
        tab0_s[6:7, h * 128 : h * 128 + 128] = mass_ref[h : h + 1, :]
    for h2 in range(groups // 2):
        two = jnp.concatenate(
            [tab0_s[:, h2 * 512 : h2 * 512 + 256], tab0_s[:, h2 * 512 + 256 : h2 * 512 + 512]], axis=0
        )
        hi, lo = split2(two)
        tabm_s[h2 * 16 : h2 * 16 + 16, 0:256] = hi
        tabm_s[h2 * 16 : h2 * 16 + 16, 256:512] = lo

    width = 512

    def pick_state(g, carry):
        idx = lanes_of_rows(conn_s, 4 * g, 4)
        oh = one_hot(jnp.bitwise_and(idx, 255), width)
        res = jnp.dot(
            tabm_s[...], jnp.concatenate([oh, oh], axis=0), preferred_element_type=F32
        )
        hb = jnp.broadcast_to(lax.shift_right_logical(idx, 8), (8, width))
        acc = jnp.zeros((8, width), F32)
        for h in range(groups):
            acc = jnp.where(hb == h, res[8 * h : 8 * h + 8], acc)
        for q in range(4):
            st_s[pl.ds(4 * g + q, 8, stride=128), :] = acc[:, 128 * q : 128 * q + 128]
        return carry

    lax.fori_loop(0, 32, pick_state, 0, unroll=2)

    absorb = absorb_ref[...].astype(F32)
    retain = jnp.exp(-DT * damp_ref[...])
    m_s[...] = jnp.zeros(m_s.shape, F32)
    for d in range(3):
        for c in range(3):
            m_s[d * 128 : d * 128 + 125, c * 128 : c * 128 + 128] = mem_ref[3 * d + c]
    row = lax.broadcasted_iota(jnp.int32, (128, 128), 0)
    mass = st_s[768:896, :]
    st_s[896:1024, :] = jnp.where(row < 125, DT / jnp.where(row < 125, mass, 1.0), 0.0)
    acc_s[...] = jnp.zeros(acc_s.shape, F32)

    for copy in kcopies:
        copy.wait()
    true = jnp.full((128, 128), True)
    for d, (low_point, high_point) in enumerate(((12, 112), (52, 72), (60, 64))):
        low = conn_s[low_point : low_point + 1, :]
        high = conn_s[high_point : high_point + 1, :]
        mat_s[2 * d, 0:128, :] = match(column(high), low, true)
        mat_s[2 * d + 1, 0:128, :] = match(column(low), high, true)
        if d < 2:
            pos, count = ((slab, n_slab), (sec, n_sec))[d]
            low_k = kown_s[2 * d : 2 * d + 1, :]
            high_k = kown_s[2 * d + 1 : 2 * d + 2, :]
            from_prev = column(kgot_s[2 * d, 2 * d + 1 : 2 * d + 2, :])
            from_next = column(kgot_s[2 * d + 1, 2 * d : 2 * d + 1, :])
            mat_s[2 * d, 128:256, :] = match(from_prev, low_k, (low_k > 0.5) & (pos > 0))
            mat_s[2 * d + 1, 128:256, :] = match(
                from_next, high_k, (high_k > 0.5) & (pos < count - 1)
            )

    def local_sum(d):
        take_face(f_s, 2 * d, fa_s)
        take_face(f_s, 2 * d + 1, fb_s)
        into_low = dot3(fb_s[...], mat_s[2 * d, 0:128, :])
        into_high = dot3(fa_s[...], mat_s[2 * d + 1, 0:128, :])
        add_face(f_s, 2 * d, into_low)
        add_face(f_s, 2 * d + 1, into_high)

    fa_s[...] = jnp.zeros(fa_s.shape, F32)
    fb_s[...] = jnp.zeros(fb_s.shape, F32)
    send_s[...] = jnp.zeros(send_s.shape, F32)
    f_s[...] = jnp.ones(f_s.shape, F32)
    for d in range(3):
        local_sum(d)
    w_s[...] = 1.0 / f_s[0:128, :]

    def element_force():
        u = jnp.concatenate([st_s[c * 128 : c * 128 + 128, :] for c in range(3)], axis=1)
        g = jnp.dot(grad_ref[...], u, precision=HIGHEST, preferred_element_type=F32)
        wide = lambda x: jnp.concatenate([x, x, x], axis=1)
        ab, rt = wide(absorb), wide(retain)
        weight = wide(mod_ref[...] * cube_ref[...])
        weight = jnp.concatenate([weight, weight, weight], axis=0)
        mem = m_s[...]
        stress = weight * (g - ab * mem)
        m_s[...] = ab * (rt * mem + (1.0 - rt) * g)
        div = jnp.dot(gradt_ref[...], stress, precision=HIGHEST, preferred_element_type=F32)
        for c in range(3):
            f_s[c * 128 : c * 128 + 128, :] = -div[:, c * 128 : c * 128 + 128]

    element_force()

    p = paired(fp_ref)
    pf = p.astype(F32)
    a = ((pf + 0.5) * (1.0 / 1536.0)).astype(jnp.int32)
    n = p - a * 1536
    s = ((n.astype(F32) + 0.5) * (1.0 / 12.0)).astype(jnp.int32)
    c = n - s * 12
    h_s[...] = jnp.where(p >= 12288, 1000, c * 4 + lax.shift_right_logical(a, 1))
    lo_s[...] = jnp.bitwise_and(a, 1) * 128 + s
    fn_s[...] = paired(fn_ref)

    many = pl.ds(0, (devices - 1) * 9)
    pltpu.make_async_copy(rows_send.at[many], rows_got.at[many], rsem_recv).wait()
    blocks = [rows_got[pl.ds(j, 128, stride=16), :].T for j in range(9)]
    blocks = jnp.concatenate(blocks, axis=0)
    for c in range(12):
        base = c * 96
        hi, lo = split2(halves(blocks[base : base + 48], blocks[base + 48 : base + 96]))
        tabp_s[c * 48 : c * 48 + 48, 0:256] = hi
        tabp_s[c * 48 : c * 48 + 48, 256:512] = lo
    sub12 = lax.broadcasted_iota(jnp.int32, (48, width), 0) // 12
    lane = lax.broadcasted_iota(jnp.int32, (8, 128), 1)

    def send_points(d):
        @pl.when(d != me)
        def _():
            pltpu.make_async_remote_copy(
                src_ref=pts_send.at[pl.ds(d * 8, 8)],
                dst_ref=pts_got.at[pl.ds(me * 8, 8)],
                send_sem=psem_send,
                recv_sem=psem_recv,
                device_id=place(d),
                device_id_type=MESH,
            ).start()

    def pick_points(k, carry):
        g = lax.rem(k + me, 16)
        oh = one_hot(lanes_of_rows(lo_s, 4 * g, 4), width)
        res = jnp.dot(
            tabp_s[...], jnp.concatenate([oh, oh], axis=0), preferred_element_type=F32
        )
        hb = jnp.broadcast_to(lanes_of_rows(h_s, 4 * g, 4), (48, width)) - sub12
        acc = jnp.zeros((48, width), F32)
        for q in range(12):
            acc = jnp.where(hb == 4 * q, res[48 * q : 48 * q + 48], acc)
        acc = acc[0:24] + acc[24:48]
        acc = acc[0:12] + acc[12:24]
        x = acc[0:8]
        y = jnp.concatenate([acc[8:12], acc[8:12]], axis=0)
        for q in range(4):
            xq = x[:, 128 * q : 128 * q + 128]
            yq = y[:, 128 * q : 128 * q + 128]
            r = (4 * g + q) * 8
            pts_send[pl.ds(pl.multiple_of(r, 8), 8), :] = jnp.where(lane < 64, xq, pltpu.roll(yq, 64, 1))
            pts_send[pl.ds(pl.multiple_of(r + 512, 8), 8), :] = jnp.where(
                lane < 64, pltpu.roll(xq, 64, 1), yq
            )
        for q in range(4):
            send_points(4 * g + q)
            send_points(4 * g + q + 64)
        return carry

    lax.fori_loop(0, 16, pick_points, 0)
    own = pl.ds(pl.multiple_of(me * 8, 8), 8)
    pts_got[own, :] = pts_send[own, :]
    many = pl.ds(0, (devices - 1) * 8)
    pltpu.make_async_copy(pts_send.at[many], pts_got.at[many], psem_recv).wait()

    dep_s[...] = jnp.zeros(dep_s.shape, F32)

    def deposit(g, carry):
        vals = []
        for q in range(4):
            r = (4 * g + q) * 8
            c0 = pts_got[pl.ds(pl.multiple_of(r, 8), 8), :]
            c1 = pts_got[pl.ds(pl.multiple_of(r + 512, 8), 8), :]
            x = jnp.where(lane < 64, c0, pltpu.roll(c1, 64, 1))
            y = jnp.where(lane < 64, pltpu.roll(c0, 64, 1), c1)
            v12 = jnp.concatenate([x, y[0:4]], axis=0)
            v24 = jnp.concatenate([v12, v12], axis=0)
            vals.append(jnp.concatenate([v24, v24], axis=0))
        vhi, vlo = split2(jnp.concatenate(vals, axis=1))
        idx = lanes_of_rows(fn_s, 4 * g, 4)
        idx = jnp.where(idx >= nodes, 1 << 20, idx)
        oh = one_hot(jnp.bitwise_and(idx, 255), width)
        high = jnp.minimum(lax.shift_right_logical(idx, 8), 200)
        hb = (jnp.broadcast_to(high, (48, width)) - sub12).astype(F32).astype(BF16)
        zero = jnp.zeros((48, width), BF16)
        lhs = []
        for q in range(10):
            mask = hb == jnp.asarray(4 * q, BF16)
            lhs.append(halves(jnp.where(mask, vhi, zero), jnp.where(mask, vlo, zero)))
        res = lax.dot_general(
            jnp.concatenate(lhs, axis=0),
            halves(oh, oh),
            (((1,), (1,)), ((), ())),
            preferred_element_type=F32,
        )
        dep_s[0] += res[:, 0:128]
        dep_s[1] += res[:, 128:256]
        return carry

    lax.fori_loop(0, 16, deposit, 0)

    for n in range(4):
        sides = []
        for side in range(2):
            parts = [dep_s[side, pl.ds(3 * n + c, 40, stride=12), :] for c in range(3)]
            sides.append(jnp.concatenate(parts + [jnp.zeros((8, 128), F32)], axis=0))
        hi, lo = split2(halves(sides[0], sides[1]))
        tabi_s[n, :, 0:256] = hi
        tabi_s[n, :, 256:512] = lo
    sub = lax.broadcasted_iota(jnp.int32, (8, width), 0)

    def pick_inj(n, g):
        idx = lanes_of_rows(conn_s, 4 * g, 4)
        oh = one_hot(jnp.bitwise_and(idx, 255), width)
        res = jnp.dot(
            tabi_s[n], jnp.concatenate([oh, oh], axis=0), preferred_element_type=F32
        )
        hb = jnp.broadcast_to(lax.shift_right_logical(idx, 8), (8, width)) - sub
        acc = [jnp.zeros((8, width), F32)] * 3
        for q in range(5):
            mask = hb == 8 * q
            for c in range(3):
                at = 40 * c + 8 * q
                acc[c] = jnp.where(mask, res[at : at + 8], acc[c])
        for c in range(3):
            total = jnp.sum(acc[c], axis=0, keepdims=True)
            for q in range(4):
                ie_s[pl.ds(n * 384 + c * 128 + 4 * g + q, 1), :] = total[:, 128 * q : 128 * q + 128]

    def pick_injs(n, start, stop):
        def body(g, carry):
            pick_inj(n, g)
            return carry

        lax.fori_loop(start, stop, body, 0, unroll=2)

    pick_injs(0, 0, 32)

    def step(n, carry):
        for c in range(3):
            at = slice(c * 128, c * 128 + 128)
            inj = ie_s[pl.ds(pl.multiple_of(n * 384 + c * 128, 128), 128), :]
            f_s[at, :] = f_s[at, :] + w_s[...] * inj
        for d in range(2):
            sends = []
            for side in range(2):
                part = 2 * d + side
                take_face(f_s, part, send_s.at[part])
            for side in range(2):
                part = 2 * d + side
                copy = pltpu.make_async_remote_copy(
                    src_ref=send_s.at[part],
                    dst_ref=recv_s.at[n, part ^ 1],
                    send_sem=sem_send.at[n, part],
                    recv_sem=sem_recv.at[n, part ^ 1],
                    device_id=targets[part],
                    device_id_type=MESH,
                )
                copy.start()
                sends.append(copy)
            into_low = dot3(send_s[2 * d + 1], mat_s[2 * d, 0:128, :])
            into_high = dot3(send_s[2 * d], mat_s[2 * d + 1, 0:128, :])

            @pl.when(n < 3)
            def _():
                pick_injs(n + 1, 16 * d, 16 * d + 16)

            for copy in sends:
                copy.wait()
            into_low += dot3(recv_s[n, 2 * d], mat_s[2 * d, 128:256, :])
            into_high += dot3(recv_s[n, 2 * d + 1], mat_s[2 * d + 1, 128:256, :])
            add_face(f_s, 2 * d, into_low)
            add_face(f_s, 2 * d + 1, into_high)
        local_sum(2)
        total = f_s[...]
        scale = st_s[896:1024, :]
        scale = jnp.concatenate([scale, scale, scale], axis=0)
        v = st_s[384:768, :] + total * scale
        st_s[384:768, :] = v
        st_s[0:384, :] = st_s[0:384, :] + DT * v
        w3 = jnp.concatenate([w_s[...], w_s[...], w_s[...]], axis=0)
        own = w3 * (total - ie_s[pl.ds(pl.multiple_of(n * 384, 128), 384), :])
        acc_s[0:384, :] = acc_s[0:384, :] + own
        acc_s[384:768, :] = acc_s[384:768, :] + (4 - n).astype(F32) * own

        @pl.when(n < 3)
        def _():
            element_force()

        return carry

    lax.fori_loop(0, 4, step, 0)

    val_s[...] = jnp.zeros(val_s.shape, F32)
    sub8 = lax.broadcasted_iota(jnp.int32, (16, width), 0) // 8

    def collect(g, carry):
        idx = lanes_of_rows(conn_s, 4 * g, 4)
        vals = []
        for q in range(4):
            six = acc_s[pl.ds(4 * g + q, 8, stride=128), :]
            vals.append(jnp.concatenate([six, six], axis=0))
        vhi, vlo = split2(jnp.concatenate(vals, axis=1))
        oh = one_hot(jnp.bitwise_and(idx, 255), width)
        high = jnp.minimum(lax.shift_right_logical(idx, 8), 200)
        hb = (jnp.broadcast_to(high, (16, width)) - sub8).astype(F32).astype(BF16)
        zero = jnp.zeros((16, width), BF16)
        lhs = []
        for q in range(groups // 2):
            mask = hb == jnp.asarray(2 * q, BF16)
            lhs.append(halves(jnp.where(mask, vhi, zero), jnp.where(mask, vlo, zero)))
        lhs = jnp.concatenate(lhs, axis=0)
        val_s[...] += lax.dot_general(
            lhs, halves(oh, oh), (((1,), (1,)), ((), ())), preferred_element_type=F32
        )
        return carry

    lax.fori_loop(0, 32, collect, 0, unroll=2)

    for h in range(nodes // 128):
        at = slice(h * 128, h * 128 + 128)
        lanes = slice((h % 2) * 128, (h % 2) * 128 + 128)
        big = h // 2
        inv = DT / mass_ref[h : h + 1, :]
        inj = [dep_s[h % 2, 12 * big + 3 * n : 12 * big + 3 * n + 3, :] for n in range(4)]
        vsum = inj[0] + inj[1] + inj[2] + inj[3] + val_s[8 * big : 8 * big + 3, lanes]
        usum = 4.0 * inj[0] + 3.0 * inj[1] + 2.0 * inj[2] + inj[3] + val_s[8 * big + 3 : 8 * big + 6, lanes]
        v0 = veloc_ref[:, at]
        outv_ref[:, at] = v0 + inv * vsum
        outd_ref[:, at] = disp_ref[:, at] + (4.0 * DT) * v0 + (DT * inv) * usum

    many = pl.ds(0, (devices - 1) * 9)
    pltpu.make_async_copy(rows_send.at[many], rows_got.at[many], rsem_send).wait()
    many = pl.ds(0, (devices - 1) * 8)
    pltpu.make_async_copy(pts_send.at[many], pts_got.at[many], psem_send).wait()


def local(n_slab, n_sec):
    grad, gradt, cube = gll_tables()
    vmem = pl.BlockSpec(memory_space=pltpu.VMEM)

    def run(
        coefficients,
        azimuths,
        route_rows,
        face_points,
        face_nodes,
        disp_start,
        veloc_start,
        memory_start,
        connectivity,
        x_shared,
        y_shared,
        absorbing,
        damping,
        modulus,
        masses,
    ):
        devices = n_slab * n_sec
        rows = azimuths.shape[1]
        nodes = disp_start.shape[1]
        groups = -(-nodes // 256)
        dma = pltpu.SemaphoreType.DMA
        return pl.pallas_call(
            lambda *refs: mega_kernel(n_slab, n_sec, *refs),
            out_shape=(
                jax.ShapeDtypeStruct((3, nodes), F32),
                jax.ShapeDtypeStruct((3, nodes), F32),
            ),
            in_specs=[vmem] * 18,
            out_specs=(vmem, vmem),
            scratch_shapes=[
                pltpu.VMEM((256, rows), BF16),
                pltpu.VMEM((devices * 16, 128), F32),
                pltpu.VMEM((devices * 16, 128), F32),
                pltpu.VMEM((devices * 8, 128), F32),
                pltpu.VMEM((devices * 8, 128), F32),
                pltpu.VMEM((576, 512), BF16),
                pltpu.VMEM((64, 128), jnp.int32),
                pltpu.VMEM((64, 128), jnp.int32),
                pltpu.VMEM((64, 128), jnp.int32),
                pltpu.VMEM((128, 128), jnp.int32),
                pltpu.VMEM((8, 640), jnp.int32),
                pltpu.VMEM((8, groups * 256), F32),
                pltpu.VMEM((groups * 8, 512), BF16),
                pltpu.VMEM((4, 128, 512), BF16),
                pltpu.VMEM((1024, 128), F32),
                pltpu.VMEM((1536, 128), F32),
                pltpu.VMEM((384, 384), F32),
                pltpu.VMEM((2, 480, 128), F32),
                pltpu.VMEM((groups * 8, 256), F32),
                pltpu.VMEM((384, 128), F32),
                pltpu.VMEM((96, 128), F32),
                pltpu.VMEM((96, 128), F32),
                pltpu.VMEM((128, 128), F32),
                pltpu.VMEM((1024, 128), F32),
                pltpu.VMEM((6, 256, 128), BF16),
                pltpu.VMEM((8, 128), F32),
                pltpu.VMEM((4, 8, 128), F32),
                pltpu.VMEM((4, 96, 128), F32),
                pltpu.VMEM((4, 4, 96, 128), F32),
                dma((4,)),
                dma((4,)),
                dma((4, 4)),
                dma((4, 4)),
                dma,
                dma,
                dma,
                dma,
            ],
            compiler_params=pltpu.CompilerParams(
                vmem_limit_bytes=VMEM_LIMIT, collective_id=0, has_side_effects=True
            ),
            name="slab_window",
        )(
            coefficients,
            azimuths,
            jnp.transpose(route_rows, (2, 0, 1)),
            face_points[0].T,
            face_nodes[0].T,
            disp_start,
            veloc_start,
            memory_start,
            connectivity,
            x_shared,
            y_shared,
            absorbing.reshape(1, -1),
            damping.reshape(1, -1),
            modulus.reshape(1, -1),
            masses.reshape(-1, 128),
            grad,
            gradt,
            cube,
        )

    return run


def solution(mesh):
    both = ("slab", "sec")
    return jax.shard_map(
        local(mesh.shape["slab"], mesh.shape["sec"]),
        mesh=mesh,
        in_specs=(
            P(None, None, both),
            P(None, both),
            P(both, None, None),
            P(both, None, None),
            P(both, None, None),
            P(None, both),
            P(None, both),
            P(None, None, both),
            P(None, both),
            P(None, both),
            P(None, both),
            P(both),
            P(both),
            P(both),
            P(both),
        ),
        out_specs=(P(None, both), P(None, both)),
        check_vma=False,
    )
```

time: 174 us -> 105 us (0.60)
  waiting for transfers between devices: 31 us -> 0 us
  starting transfers between devices: 16.1 us -> 0 us
  Pallas kernels: 117 us -> 101 us
  local copies, waits for them, and re-layouts: 8.5 us -> 3.2 us
    all_to_all x2 -> x0, waiting for transfers between devices: 31 us -> none  [the longest x1 18.5 us: run(): lax.all_to_all(payload.reshape(devices, 16, 128), ('slab', 'sec'), split_...]
    all_to_all x2 -> x0, starting transfers between devices: 16.1 us -> none  [the longest x1 11.5 us: run(): lax.all_to_all(payload.reshape(devices, 16, 128), ('slab', 'sec'), split_...]
    pallas_call x3 -> x1, Pallas kernels: 117 us -> 101 us  [run(): pl.pallas_call(lambda *refs: mega_kernel(n_slab, n_sec, *refs), out_shape...]
    unnamed x15 -> x2, local copies, waits for them, and re-layouts: 7.86 us -> 3.2 us
  transfers between devices with their start and end apart: 2 -> 0, of which waited for: 2 -> 0; matrix products, arithmetic and copies ran while one was open for 1% -> 0% of each run, Pallas kernels for 0% -> 0%
where the time goes in v1:
time: 105 us
  Pallas kernels  101 us (96%)
  local copies, waits for them, and re-layouts  3.2 us (3%)
    pallas_call x1, Pallas kernels, run(): pl.pallas_call(lambda *refs: mega_kernel(n_slab, n_sec, *refs), out_shape...  101 us
    unnamed x2, local copies, waits for them, and re-layouts  3.2 us

profile of v1, /device:TPU:1, one launch (start us, length us, event | category | flops | bytes accessed | tf_op | source)
XLA Modules:
  0.0 105.1 jit_solution(15121724698685535688)
XLA Ops:
  0.6 101.3 %slab_window.1 = (f32[3,9600]{1,0:T(4,128)}, f32[3,9600]{1,0:T(4,128)}) custom-call(f32[17,12,1152]{2,1,0:T(8,128)} %refs_0_.1, f32[8,1152]{1,0:T(8,128)} %refs_1_.1, s32[12,1,128]{2,1,0:T(1,128)} %bitcast.14, s32[64,128]{1,0:T(8,128)} %bitcast.12, s32[64,128]{1,0:T(8,128)} %bitcast.13, f32[3,9600]{1,0:T(4,128)} %refs_5_.1, f32[3,9600]{1,0:T(4,128)} %refs_6_.1, ...), custom_call_target="tpu_custom_call" | custom-call | tf_op jit(solution)/shard_map/slab_window/pallas_call | solution.py:650
  101.9 1.6 %copy.22 = f32[3,9600]{1,0:T(4,128)} copy(f32[3,9600]{1,0:T(4,128)} %get-tuple-element.4) | data formatting | bytes 230400
  103.5 1.6 %copy.23 = f32[3,9600]{1,0:T(4,128)} copy(f32[3,9600]{1,0:T(4,128)} %get-tuple-element.5) | data formatting | bytes 230400

commit v2 on v1

--- a/solution.py
+++ b/solution.py
@@ -37,7 +37,16 @@
     grad = grad.reshape(384, 128).astype(np.float32)
     cube128 = np.zeros((128, 128), np.float32)
     cube128[:125] = cube.reshape(125, 1)
-    return grad, np.ascontiguousarray(grad.T), cube128
+
+    def terms(x):
+        hi = x.astype(jnp.bfloat16)
+        return hi, (x - hi.astype(np.float32)).astype(jnp.bfloat16)
+
+    return (
+        np.concatenate(terms(grad), axis=1),
+        np.concatenate(terms(np.ascontiguousarray(grad.T)), axis=0),
+        cube128,
+    )
 
 
 def split2(x):
@@ -93,13 +102,20 @@
             f_ref[at, :] = f_ref[at, :] + vals[c * 32 + dst : c * 32 + dst + count, :]
 
 
+def dot2(x, mat):
+    parts = jnp.concatenate(split2(x), axis=0)
+    n = x.shape[0]
+    res = jnp.dot(parts, mat, preferred_element_type=F32)
+    return res[0:n] + res[n : 2 * n]
+
+
 def dot3(x, mat):
     hi = x.astype(BF16)
     rest = x - hi.astype(F32)
     mid, low = split2(rest)
-    parts = jnp.concatenate([hi, mid, low], axis=0)
+    parts = jnp.concatenate([hi.astype(F32), mid.astype(F32), low.astype(F32)], axis=0)
     n = x.shape[0]
-    res = jnp.dot(parts, mat, preferred_element_type=F32)
+    res = jnp.dot(parts.astype(BF16), mat, preferred_element_type=F32)
     return res[0:n] + res[n : 2 * n] + res[2 * n : 3 * n]
 
 
@@ -205,9 +221,14 @@
     acc_s,
     mat_s,
     kown_s,
-    kgot_s,
+    pack_s,
+    spread_s,
+    face_s,
     send_s,
     recv_s,
+    kd_s,
+    kdgot_s,
+    dia_s,
     ksem_send,
     ksem_recv,
     sem_send,
@@ -228,6 +249,7 @@
     nxt_y = lax.rem(sec + 1, n_sec)
     prv_y = lax.rem(sec + n_sec - 1, n_sec)
     targets = [(prv_x, sec), (nxt_x, sec), (slab, prv_y), (slab, nxt_y)]
+    corners = [(x, y) for x in (prv_x, nxt_x) for y in (prv_y, nxt_y)]
 
     def place(d):
         return (d // n_sec, lax.rem(d, n_sec))
@@ -276,18 +298,35 @@
             slot = lax.broadcasted_iota(jnp.int32, (128, 128), 0) + (b * 128 + 1)
             best = jnp.maximum(best, jnp.where(col == centre, slot, 0))
         kown_s[r : r + 1, :] = jnp.max(best, axis=0, keepdims=True).astype(F32)
-    kcopies = []
-    for d, dev in enumerate(targets):
+    lane1 = lax.broadcasted_iota(jnp.int32, (128, 128), 1).astype(F32)
+    row1 = lax.broadcasted_iota(jnp.int32, (128, 128), 0).astype(F32)
+    insides = (slab > 0, slab < n_slab - 1, sec > 0, sec < n_sec - 1)
+    for r in range(4):
+        slots = kown_s[r : r + 1, :]
+        col = column(slots)
+        before = jnp.where((col < slots) & (col > 0.5), 1.0, 0.0)
+        rank = jnp.sum(before, axis=0, keepdims=True)
+        rank = jnp.where(slots > 0.5, rank, -1000.0)
+        ranks = column(rank)
+        for b in range(4):
+            pack_s[r, b * 128 : b * 128 + 128, :] = match(ranks + 32.0 * b, lane1, lane1 >= 0.0)
+            spread_s[r, :, b * 128 : b * 128 + 128] = match(row1, rank + 32.0 * b, insides[r])
+
+    for a in range(2):
+        ky = dot3(kown_s[...], pack_s[a, 0:128, :])
+        kd_s[4 * a : 4 * a + 4, :] = ky[2:6]
+    dcopies = []
+    for d in (2, 3):
         copy = pltpu.make_async_remote_copy(
-            src_ref=kown_s,
-            dst_ref=kgot_s.at[d ^ 1],
+            src_ref=kd_s,
+            dst_ref=kdgot_s.at[d ^ 1],
             send_sem=ksem_send.at[d],
             recv_sem=ksem_recv.at[d ^ 1],
-            device_id=dev,
+            device_id=targets[d],
             device_id_type=MESH,
         )
         copy.start()
-        kcopies.append(copy)
+        dcopies.append(copy)
 
     tab0_s[...] = jnp.zeros(tab0_s.shape, F32)
     tab0_s[0:3, 0:nodes] = disp_ref[...]
@@ -320,6 +359,12 @@
 
     lax.fori_loop(0, 32, pick_state, 0, unroll=2)
 
+    for d, (low_point, high_point) in enumerate(((12, 112), (52, 72), (60, 64))):
+        low = conn_s[low_point : low_point + 1, :]
+        high = conn_s[high_point : high_point + 1, :]
+        mat_s[2 * d] = match(column(high), low, True)
+        mat_s[2 * d + 1] = match(column(low), high, True)
+
     absorb = absorb_ref[...].astype(F32)
     retain = jnp.exp(-DT * damp_ref[...])
     m_s[...] = jnp.zeros(m_s.shape, F32)
@@ -331,36 +376,17 @@
     st_s[896:1024, :] = jnp.where(row < 125, DT / jnp.where(row < 125, mass, 1.0), 0.0)
     acc_s[...] = jnp.zeros(acc_s.shape, F32)
 
-    for copy in kcopies:
-        copy.wait()
-    true = jnp.full((128, 128), True)
-    for d, (low_point, high_point) in enumerate(((12, 112), (52, 72), (60, 64))):
-        low = conn_s[low_point : low_point + 1, :]
-        high = conn_s[high_point : high_point + 1, :]
-        mat_s[2 * d, 0:128, :] = match(column(high), low, true)
-        mat_s[2 * d + 1, 0:128, :] = match(column(low), high, true)
-        if d < 2:
-            pos, count = ((slab, n_slab), (sec, n_sec))[d]
-            low_k = kown_s[2 * d : 2 * d + 1, :]
-            high_k = kown_s[2 * d + 1 : 2 * d + 2, :]
-            from_prev = column(kgot_s[2 * d, 2 * d + 1 : 2 * d + 2, :])
-            from_next = column(kgot_s[2 * d + 1, 2 * d : 2 * d + 1, :])
-            mat_s[2 * d, 128:256, :] = match(from_prev, low_k, (low_k > 0.5) & (pos > 0))
-            mat_s[2 * d + 1, 128:256, :] = match(
-                from_next, high_k, (high_k > 0.5) & (pos < count - 1)
-            )
-
     def local_sum(d):
         take_face(f_s, 2 * d, fa_s)
         take_face(f_s, 2 * d + 1, fb_s)
-        into_low = dot3(fb_s[...], mat_s[2 * d, 0:128, :])
-        into_high = dot3(fa_s[...], mat_s[2 * d + 1, 0:128, :])
+        into_low = dot2(fb_s[...], mat_s[2 * d])
+        into_high = dot2(fa_s[...], mat_s[2 * d + 1])
         add_face(f_s, 2 * d, into_low)
         add_face(f_s, 2 * d + 1, into_high)
 
     fa_s[...] = jnp.zeros(fa_s.shape, F32)
     fb_s[...] = jnp.zeros(fb_s.shape, F32)
-    send_s[...] = jnp.zeros(send_s.shape, F32)
+    face_s[...] = jnp.zeros(face_s.shape, F32)
     f_s[...] = jnp.ones(f_s.shape, F32)
     for d in range(3):
         local_sum(d)
@@ -368,7 +394,12 @@
 
     def element_force():
         u = jnp.concatenate([st_s[c * 128 : c * 128 + 128, :] for c in range(3)], axis=1)
-        g = jnp.dot(grad_ref[...], u, precision=HIGHEST, preferred_element_type=F32)
+        uhi, ulo = split2(u)
+        both = halves(uhi, ulo)
+        both = jnp.dot(
+            grad_ref[...], jnp.concatenate([both, both], axis=0), preferred_element_type=F32
+        )
+        g = both[:, 0:384] + both[:, 384:768]
         wide = lambda x: jnp.concatenate([x, x, x], axis=1)
         ab, rt = wide(absorb), wide(retain)
         weight = wide(mod_ref[...] * cube_ref[...])
@@ -376,7 +407,10 @@
         mem = m_s[...]
         stress = weight * (g - ab * mem)
         m_s[...] = ab * (rt * mem + (1.0 - rt) * g)
-        div = jnp.dot(gradt_ref[...], stress, precision=HIGHEST, preferred_element_type=F32)
+        shi, slo = split2(stress)
+        both = jnp.dot(gradt_ref[...], halves(shi, slo), preferred_element_type=F32)
+        both = both[:, 0:384] + both[:, 384:768]
+        div = both[0:128] + both[128:256]
         for c in range(3):
             f_s[c * 128 : c * 128 + 128, :] = -div[:, c * 128 : c * 128 + 128]
 
@@ -444,6 +478,16 @@
         return carry
 
     lax.fori_loop(0, 16, pick_points, 0)
+    for copy in dcopies:
+        copy.wait()
+    for a in range(2):
+        for b in range(2):
+            slots = column(kdgot_s[2 + b, 4 * a + 1 - b : 4 * a + 2 - b, :])
+            mine = kown_s[2 + b : 3 + b, :]
+            good = (mine > 0.5) & insides[a] & insides[2 + b]
+            for q in range(4):
+                moved = slots if q == 0 else pltpu.roll(slots, 32 * q, 0)
+                dia_s[2 * a + b, :, q * 128 : q * 128 + 128] = match(moved, mine, good)
     own = pl.ds(pl.multiple_of(me * 8, 8), 8)
     pts_got[own, :] = pts_send[own, :]
     many = pl.ds(0, (devices - 1) * 8)
@@ -469,21 +513,17 @@
         high = jnp.minimum(lax.shift_right_logical(idx, 8), 200)
         hb = (jnp.broadcast_to(high, (48, width)) - sub12).astype(F32).astype(BF16)
         zero = jnp.zeros((48, width), BF16)
-        lhs = []
-        for q in range(10):
-            mask = hb == jnp.asarray(4 * q, BF16)
-            lhs.append(halves(jnp.where(mask, vhi, zero), jnp.where(mask, vlo, zero)))
+        masks = [hb == jnp.asarray(4 * q, BF16) for q in range(10)]
+        lhs = [jnp.where(mask, v, zero) for v in (vhi, vlo) for mask in masks]
         res = lax.dot_general(
-            jnp.concatenate(lhs, axis=0),
-            halves(oh, oh),
-            (((1,), (1,)), ((), ())),
-            preferred_element_type=F32,
+            jnp.concatenate(lhs, axis=0), oh, (((1,), (1,)), ((), ())), preferred_element_type=F32
         )
+        res = res[0:480] + res[480:960]
         dep_s[0] += res[:, 0:128]
         dep_s[1] += res[:, 128:256]
         return carry
 
-    lax.fori_loop(0, 16, deposit, 0)
+    lax.fori_loop(0, 16, deposit, 0, unroll=2)
 
     for n in range(4):
         sides = []
@@ -491,16 +531,15 @@
             parts = [dep_s[side, pl.ds(3 * n + c, 40, stride=12), :] for c in range(3)]
             sides.append(jnp.concatenate(parts + [jnp.zeros((8, 128), F32)], axis=0))
         hi, lo = split2(halves(sides[0], sides[1]))
-        tabi_s[n, :, 0:256] = hi
-        tabi_s[n, :, 256:512] = lo
+        tabi_s[n, 0:128, :] = hi
+        tabi_s[n, 128:256, :] = lo
     sub = lax.broadcasted_iota(jnp.int32, (8, width), 0)
 
     def pick_inj(n, g):
         idx = lanes_of_rows(conn_s, 4 * g, 4)
         oh = one_hot(jnp.bitwise_and(idx, 255), width)
-        res = jnp.dot(
-            tabi_s[n], jnp.concatenate([oh, oh], axis=0), preferred_element_type=F32
-        )
+        res = jnp.dot(tabi_s[n], oh, preferred_element_type=F32)
+        res = res[0:120] + res[128:248]
         hb = jnp.broadcast_to(lax.shift_right_logical(idx, 8), (8, width)) - sub
         acc = [jnp.zeros((8, width), F32)] * 3
         for q in range(5):
@@ -527,37 +566,45 @@
             at = slice(c * 128, c * 128 + 128)
             inj = ie_s[pl.ds(pl.multiple_of(n * 384 + c * 128, 128), 128), :]
             f_s[at, :] = f_s[at, :] + w_s[...] * inj
-        for d in range(2):
-            sends = []
-            for side in range(2):
-                part = 2 * d + side
-                take_face(f_s, part, send_s.at[part])
-            for side in range(2):
-                part = 2 * d + side
-                copy = pltpu.make_async_remote_copy(
-                    src_ref=send_s.at[part],
-                    dst_ref=recv_s.at[n, part ^ 1],
-                    send_sem=sem_send.at[n, part],
-                    recv_sem=sem_recv.at[n, part ^ 1],
-                    device_id=targets[part],
-                    device_id_type=MESH,
-                )
-                copy.start()
-                sends.append(copy)
-            into_low = dot3(send_s[2 * d + 1], mat_s[2 * d, 0:128, :])
-            into_high = dot3(send_s[2 * d], mat_s[2 * d + 1, 0:128, :])
-
-            @pl.when(n < 3)
-            def _():
-                pick_injs(n + 1, 16 * d, 16 * d + 16)
-
-            for copy in sends:
-                copy.wait()
-            into_low += dot3(recv_s[n, 2 * d], mat_s[2 * d, 128:256, :])
-            into_high += dot3(recv_s[n, 2 * d + 1], mat_s[2 * d + 1, 128:256, :])
-            add_face(f_s, 2 * d, into_low)
-            add_face(f_s, 2 * d + 1, into_high)
-        local_sum(2)
+        for d in range(3):
+            local_sum(d)
+        sends = []
+        for part in range(4):
+            take_face(f_s, part, face_s.at[part])
+            face = jnp.concatenate([face_s[part, 24 * b : 24 * b + 24, :] for b in range(4)], axis=1)
+            send_s[part] = dot2(face, pack_s[part])
+        for part in range(8):
+            corner = part - 4
+            copy = pltpu.make_async_remote_copy(
+                src_ref=send_s.at[part if part < 4 else corner // 2],
+                dst_ref=recv_s.at[n, part ^ 1 if part < 4 else 4 + (corner ^ 3)],
+                send_sem=sem_send.at[n, part],
+                recv_sem=sem_recv.at[n, part ^ 1 if part < 4 else 4 + (corner ^ 3)],
+                device_id=targets[part] if part < 4 else corners[corner],
+                device_id_type=MESH,
+            )
+            copy.start()
+            sends.append(copy)
+
+        @pl.when(n < 3)
+        def _():
+            pick_injs(n + 1, 0, 32)
+
+        for copy in sends:
+            copy.wait()
+        into = []
+        for part in range(8):
+            mat = spread_s[part] if part < 4 else dia_s[part - 4]
+            res = dot2(recv_s[n, part], mat)
+            into.append(jnp.concatenate([res[:, 128 * b : 128 * b + 128] for b in range(4)], axis=0))
+        for part in range(4):
+            add_face(f_s, part, into[part])
+        for a in range(2):
+            for b in range(2):
+                for c in range(3):
+                    start = c * 128 + a * 100 + b * 20
+                    src = c * 32 + (1 - b) * 20
+                    f_s[start : start + 5, :] = f_s[start : start + 5, :] + into[4 + 2 * a + b][src : src + 5]
         total = f_s[...]
         scale = st_s[896:1024, :]
         scale = jnp.concatenate([scale, scale, scale], axis=0)
@@ -591,14 +638,12 @@
         high = jnp.minimum(lax.shift_right_logical(idx, 8), 200)
         hb = (jnp.broadcast_to(high, (16, width)) - sub8).astype(F32).astype(BF16)
         zero = jnp.zeros((16, width), BF16)
-        lhs = []
-        for q in range(groups // 2):
-            mask = hb == jnp.asarray(2 * q, BF16)
-            lhs.append(halves(jnp.where(mask, vhi, zero), jnp.where(mask, vlo, zero)))
-        lhs = jnp.concatenate(lhs, axis=0)
-        val_s[...] += lax.dot_general(
-            lhs, halves(oh, oh), (((1,), (1,)), ((), ())), preferred_element_type=F32
+        masks = [hb == jnp.asarray(2 * q, BF16) for q in range(groups // 2)]
+        lhs = [jnp.where(mask, v, zero) for v in (vhi, vlo) for mask in masks]
+        res = lax.dot_general(
+            jnp.concatenate(lhs, axis=0), oh, (((1,), (1,)), ((), ())), preferred_element_type=F32
         )
+        val_s[...] += res[0 : groups * 8] + res[groups * 8 : groups * 16]
         return carry
 
     lax.fori_loop(0, 32, collect, 0, unroll=2)
@@ -669,7 +714,7 @@
                 pltpu.VMEM((8, 640), jnp.int32),
                 pltpu.VMEM((8, groups * 256), F32),
                 pltpu.VMEM((groups * 8, 512), BF16),
-                pltpu.VMEM((4, 128, 512), BF16),
+                pltpu.VMEM((4, 256, 256), BF16),
                 pltpu.VMEM((1024, 128), F32),
                 pltpu.VMEM((1536, 128), F32),
                 pltpu.VMEM((384, 384), F32),
@@ -680,15 +725,20 @@
                 pltpu.VMEM((96, 128), F32),
                 pltpu.VMEM((128, 128), F32),
                 pltpu.VMEM((1024, 128), F32),
-                pltpu.VMEM((6, 256, 128), BF16),
+                pltpu.VMEM((6, 128, 128), BF16),
+                pltpu.VMEM((8, 128), F32),
+                pltpu.VMEM((4, 512, 128), BF16),
+                pltpu.VMEM((4, 128, 512), BF16),
+                pltpu.VMEM((4, 96, 128), F32),
+                pltpu.VMEM((4, 24, 128), F32),
+                pltpu.VMEM((4, 8, 24, 128), F32),
                 pltpu.VMEM((8, 128), F32),
                 pltpu.VMEM((4, 8, 128), F32),
-                pltpu.VMEM((4, 96, 128), F32),
-                pltpu.VMEM((4, 4, 96, 128), F32),
+                pltpu.VMEM((4, 128, 512), BF16),
                 dma((4,)),
                 dma((4,)),
-                dma((4, 4)),
-                dma((4, 4)),
+                dma((4, 8)),
+                dma((4, 8)),
                 dma,
                 dma,
                 dma,

time: 105 us -> 93 us (0.89)
  Pallas kernels: 101 us -> 89 us
    pallas_call x1, Pallas kernels: 101 us -> 89 us  [run(): pl.pallas_call(lambda *refs: mega_kernel(n_slab, n_sec, *refs), out_shape...]
where the time goes in v2:
time: 93 us; the launch traced here: 92.9 us
  Pallas kernels  89 us (96%)
  local copies, waits for them, and re-layouts  3.2 us (3%)
    pallas_call x1, Pallas kernels, run(): pl.pallas_call(lambda *refs: mega_kernel(n_slab, n_sec, *refs), out_shape...  89 us
    unnamed x2, local copies, waits for them, and re-layouts  3.2 us

profile of v2, /device:TPU:1, one launch (start us, length us, event | category | flops | bytes accessed | tf_op | source)
XLA Modules:
  0.0 92.9 jit_solution(13518562565292457108)
XLA Ops:
  0.6 89.0 %slab_window.1 = (f32[3,9600]{1,0:T(4,128)}, f32[3,9600]{1,0:T(4,128)}) custom-call(f32[17,12,1152]{2,1,0:T(8,128)} %refs_0_.1, f32[8,1152]{1,0:T(8,128)} %refs_1_.1, s32[12,1,128]{2,1,0:T(1,128)} %bitcast.14, s32[64,128]{1,0:T(8,128)} %bitcast.12, s32[64,128]{1,0:T(8,128)} %bitcast.13, f32[3,9600]{1,0:T(4,128)} %refs_5_.1, f32[3,9600]{1,0:T(4,128)} %refs_6_.1, ...), custom_call_target="tpu_custom_call" | custom-call | tf_op jit(solution)/shard_map/slab_window/pallas_call | solution.py:695
  89.6 1.6 %copy.22 = f32[3,9600]{1,0:T(4,128)} copy(f32[3,9600]{1,0:T(4,128)} %get-tuple-element.4) | data formatting | bytes 230400
  91.2 1.6 %copy.23 = f32[3,9600]{1,0:T(4,128)} copy(f32[3,9600]{1,0:T(4,128)} %get-tuple-element.5) | data formatting | bytes 230400

commit v3 on v2

--- a/solution.py
+++ b/solution.py
@@ -150,14 +150,18 @@
     lane = lax.broadcasted_iota(jnp.int32, (128, rows), 1)
     lane1 = lax.broadcasted_iota(jnp.int32, (128, 128), 1)
     for quad in range(3):
-        got = []
+        picks = []
         for c in range(4 * quad, 4 * quad + 4):
             col = jnp.concatenate([column(route_ref[c])] * (rows // 128), axis=1)
-            pick = jnp.where(col == lane, 1.0, 0.0).astype(BF16)
-            res = lax.dot_general(
-                pick, tr_ref[...], (((1,), (1,)), ((), ())), preferred_element_type=F32
-            )
-            got.append(res[:, :128] + res[:, 128:])
+            picks.append(jnp.where(col == lane, 1.0, 0.0).astype(BF16))
+        res = lax.dot_general(
+            jnp.concatenate(picks, axis=0),
+            tr_ref[...],
+            (((1,), (1,)), ((), ())),
+            preferred_element_type=F32,
+        )
+        res = res[:, :128] + res[:, 128:]
+        got = [res[128 * c : 128 * c + 128] for c in range(4)]
         b1 = pltpu.roll(got[1], 96, 1)
         b2 = pltpu.roll(got[2], 64, 1)
         b3 = pltpu.roll(got[3], 32, 1)
@@ -193,8 +197,8 @@
     grad_ref,
     gradt_ref,
     cube_ref,
-    outd_ref,
-    outv_ref,
+    acc_s,
+    dep_s,
     tr_s,
     rows_send,
     rows_got,
@@ -212,13 +216,10 @@
     st_s,
     ie_s,
     m_s,
-    dep_s,
-    val_s,
     f_s,
     fa_s,
     fb_s,
     w_s,
-    acc_s,
     mat_s,
     kown_s,
     pack_s,
@@ -357,7 +358,7 @@
             st_s[pl.ds(4 * g + q, 8, stride=128), :] = acc[:, 128 * q : 128 * q + 128]
         return carry
 
-    lax.fori_loop(0, 32, pick_state, 0, unroll=2)
+    lax.fori_loop(0, 32, pick_state, 0, unroll=4)
 
     for d, (low_point, high_point) in enumerate(((12, 112), (52, 72), (60, 64))):
         low = conn_s[low_point : low_point + 1, :]
@@ -442,8 +443,8 @@
         @pl.when(d != me)
         def _():
             pltpu.make_async_remote_copy(
-                src_ref=pts_send.at[pl.ds(d * 8, 8)],
-                dst_ref=pts_got.at[pl.ds(me * 8, 8)],
+                src_ref=pts_send.at[pl.ds(d * 8, 6)],
+                dst_ref=pts_got.at[pl.ds(me * 8, 6)],
                 send_sem=psem_send,
                 recv_sem=psem_recv,
                 device_id=place(d),
@@ -463,7 +464,7 @@
         acc = acc[0:24] + acc[24:48]
         acc = acc[0:12] + acc[12:24]
         x = acc[0:8]
-        y = jnp.concatenate([acc[8:12], acc[8:12]], axis=0)
+        y = jnp.concatenate([acc[6:12], acc[0:2]], axis=0)
         for q in range(4):
             xq = x[:, 128 * q : 128 * q + 128]
             yq = y[:, 128 * q : 128 * q + 128]
@@ -477,7 +478,7 @@
             send_points(4 * g + q + 64)
         return carry
 
-    lax.fori_loop(0, 16, pick_points, 0)
+    lax.fori_loop(0, 16, pick_points, 0, unroll=2)
     for copy in dcopies:
         copy.wait()
     for a in range(2):
@@ -490,7 +491,7 @@
                 dia_s[2 * a + b, :, q * 128 : q * 128 + 128] = match(moved, mine, good)
     own = pl.ds(pl.multiple_of(me * 8, 8), 8)
     pts_got[own, :] = pts_send[own, :]
-    many = pl.ds(0, (devices - 1) * 8)
+    many = pl.ds(0, (devices - 1) * 6)
     pltpu.make_async_copy(pts_send.at[many], pts_got.at[many], psem_recv).wait()
 
     dep_s[...] = jnp.zeros(dep_s.shape, F32)
@@ -503,7 +504,7 @@
             c1 = pts_got[pl.ds(pl.multiple_of(r + 512, 8), 8), :]
             x = jnp.where(lane < 64, c0, pltpu.roll(c1, 64, 1))
             y = jnp.where(lane < 64, pltpu.roll(c0, 64, 1), c1)
-            v12 = jnp.concatenate([x, y[0:4]], axis=0)
+            v12 = jnp.concatenate([x[0:6], y[0:6]], axis=0)
             v24 = jnp.concatenate([v12, v12], axis=0)
             vals.append(jnp.concatenate([v24, v24], axis=0))
         vhi, vlo = split2(jnp.concatenate(vals, axis=1))
@@ -523,7 +524,7 @@
         dep_s[1] += res[:, 128:256]
         return carry
 
-    lax.fori_loop(0, 16, deposit, 0, unroll=2)
+    lax.fori_loop(0, 16, deposit, 0, unroll=4)
 
     for n in range(4):
         sides = []
@@ -557,9 +558,21 @@
             pick_inj(n, g)
             return carry
 
-        lax.fori_loop(start, stop, body, 0, unroll=2)
+        lax.fori_loop(start, stop, body, 0, unroll=8)
 
     pick_injs(0, 0, 32)
+
+    def exchange(n, part):
+        corner = part - 4
+        into = part ^ 1 if part < 4 else 4 + (corner ^ 3)
+        return pltpu.make_async_remote_copy(
+            src_ref=send_s.at[n, part if part < 4 else corner // 2],
+            dst_ref=recv_s.at[n, into],
+            send_sem=sem_send.at[n, part],
+            recv_sem=sem_recv.at[n, into],
+            device_id=targets[part] if part < 4 else corners[corner],
+            device_id_type=MESH,
+        )
 
     def step(n, carry):
         for c in range(3):
@@ -568,32 +581,20 @@
             f_s[at, :] = f_s[at, :] + w_s[...] * inj
         for d in range(3):
             local_sum(d)
-        sends = []
         for part in range(4):
             take_face(f_s, part, face_s.at[part])
             face = jnp.concatenate([face_s[part, 24 * b : 24 * b + 24, :] for b in range(4)], axis=1)
-            send_s[part] = dot2(face, pack_s[part])
-        for part in range(8):
-            corner = part - 4
-            copy = pltpu.make_async_remote_copy(
-                src_ref=send_s.at[part if part < 4 else corner // 2],
-                dst_ref=recv_s.at[n, part ^ 1 if part < 4 else 4 + (corner ^ 3)],
-                send_sem=sem_send.at[n, part],
-                recv_sem=sem_recv.at[n, part ^ 1 if part < 4 else 4 + (corner ^ 3)],
-                device_id=targets[part] if part < 4 else corners[corner],
-                device_id_type=MESH,
-            )
-            copy.start()
-            sends.append(copy)
+            send_s[n, part] = dot2(face, pack_s[part])
+            for to in (part, 2 * part + 4, 2 * part + 5) if part < 2 else (part,):
+                exchange(n, to).start()
 
         @pl.when(n < 3)
         def _():
             pick_injs(n + 1, 0, 32)
 
-        for copy in sends:
-            copy.wait()
         into = []
         for part in range(8):
+            exchange(n, part ^ 1 if part < 4 else 4 + ((part - 4) ^ 3)).wait_recv()
             mat = spread_s[part] if part < 4 else dia_s[part - 4]
             res = dot2(recv_s[n, part], mat)
             into.append(jnp.concatenate([res[:, 128 * b : 128 * b + 128] for b in range(4)], axis=0))
@@ -623,9 +624,24 @@
         return carry
 
     lax.fori_loop(0, 4, step, 0)
+    for n in range(4):
+        for part in range(8):
+            exchange(n, part).wait_send()
+
+    many = pl.ds(0, (devices - 1) * 9)
+    pltpu.make_async_copy(rows_send.at[many], rows_got.at[many], rsem_send).wait()
+    many = pl.ds(0, (devices - 1) * 6)
+    pltpu.make_async_copy(pts_send.at[many], pts_got.at[many], psem_send).wait()
+
+
+def collect_kernel(acc_s, dep_s, conn_ref, disp_ref, veloc_ref, mass_ref, outd_ref, outv_ref, conn_s, val_s):
+    nodes = disp_ref.shape[1]
+    groups = -(-nodes // 256)
+    conn_s[...] = jnp.full(conn_s.shape, 1 << 20, jnp.int32)
+    conn_s[0:125, :] = conn_ref[...]
 
     val_s[...] = jnp.zeros(val_s.shape, F32)
-    sub8 = lax.broadcasted_iota(jnp.int32, (16, width), 0) // 8
+    sub8 = lax.broadcasted_iota(jnp.int32, (16, 512), 0) // 8
 
     def collect(g, carry):
         idx = lanes_of_rows(conn_s, 4 * g, 4)
@@ -634,10 +650,10 @@
             six = acc_s[pl.ds(4 * g + q, 8, stride=128), :]
             vals.append(jnp.concatenate([six, six], axis=0))
         vhi, vlo = split2(jnp.concatenate(vals, axis=1))
-        oh = one_hot(jnp.bitwise_and(idx, 255), width)
+        oh = one_hot(jnp.bitwise_and(idx, 255), 512)
         high = jnp.minimum(lax.shift_right_logical(idx, 8), 200)
-        hb = (jnp.broadcast_to(high, (16, width)) - sub8).astype(F32).astype(BF16)
-        zero = jnp.zeros((16, width), BF16)
+        hb = (jnp.broadcast_to(high, (16, 512)) - sub8).astype(F32).astype(BF16)
+        zero = jnp.zeros((16, 512), BF16)
         masks = [hb == jnp.asarray(2 * q, BF16) for q in range(groups // 2)]
         lhs = [jnp.where(mask, v, zero) for v in (vhi, vlo) for mask in masks]
         res = lax.dot_general(
@@ -646,7 +662,7 @@
         val_s[...] += res[0 : groups * 8] + res[groups * 8 : groups * 16]
         return carry
 
-    lax.fori_loop(0, 32, collect, 0, unroll=2)
+    lax.fori_loop(0, 32, collect, 0, unroll=8)
 
     for h in range(nodes // 128):
         at = slice(h * 128, h * 128 + 128)
@@ -659,11 +675,6 @@
         v0 = veloc_ref[:, at]
         outv_ref[:, at] = v0 + inv * vsum
         outd_ref[:, at] = disp_ref[:, at] + (4.0 * DT) * v0 + (DT * inv) * usum
-
-    many = pl.ds(0, (devices - 1) * 9)
-    pltpu.make_async_copy(rows_send.at[many], rows_got.at[many], rsem_send).wait()
-    many = pl.ds(0, (devices - 1) * 8)
-    pltpu.make_async_copy(pts_send.at[many], pts_got.at[many], psem_send).wait()
 
 
 def local(n_slab, n_sec):
@@ -692,11 +703,12 @@
         nodes = disp_start.shape[1]
         groups = -(-nodes // 256)
         dma = pltpu.SemaphoreType.DMA
-        return pl.pallas_call(
+        mass_rows = masses.reshape(-1, 128)
+        sums, injected = pl.pallas_call(
             lambda *refs: mega_kernel(n_slab, n_sec, *refs),
             out_shape=(
-                jax.ShapeDtypeStruct((3, nodes), F32),
-                jax.ShapeDtypeStruct((3, nodes), F32),
+                jax.ShapeDtypeStruct((1024, 128), F32),
+                jax.ShapeDtypeStruct((2, 480, 128), F32),
             ),
             in_specs=[vmem] * 18,
             out_specs=(vmem, vmem),
@@ -718,19 +730,16 @@
                 pltpu.VMEM((1024, 128), F32),
                 pltpu.VMEM((1536, 128), F32),
                 pltpu.VMEM((384, 384), F32),
-                pltpu.VMEM((2, 480, 128), F32),
-                pltpu.VMEM((groups * 8, 256), F32),
                 pltpu.VMEM((384, 128), F32),
                 pltpu.VMEM((96, 128), F32),
                 pltpu.VMEM((96, 128), F32),
                 pltpu.VMEM((128, 128), F32),
-                pltpu.VMEM((1024, 128), F32),
                 pltpu.VMEM((6, 128, 128), BF16),
                 pltpu.VMEM((8, 128), F32),
                 pltpu.VMEM((4, 512, 128), BF16),
                 pltpu.VMEM((4, 128, 512), BF16),
                 pltpu.VMEM((4, 96, 128), F32),
-                pltpu.VMEM((4, 24, 128), F32),
+                pltpu.VMEM((4, 4, 24, 128), F32),
                 pltpu.VMEM((4, 8, 24, 128), F32),
                 pltpu.VMEM((8, 128), F32),
                 pltpu.VMEM((4, 8, 128), F32),
@@ -763,11 +772,23 @@
             absorbing.reshape(1, -1),
             damping.reshape(1, -1),
             modulus.reshape(1, -1),
-            masses.reshape(-1, 128),
+            mass_rows,
             grad,
             gradt,
             cube,
         )
+        return pl.pallas_call(
+            collect_kernel,
+            out_shape=(
+                jax.ShapeDtypeStruct((3, nodes), F32),
+                jax.ShapeDtypeStruct((3, nodes), F32),
+            ),
+            in_specs=[vmem] * 6,
+            out_specs=(vmem, vmem),
+            scratch_shapes=[pltpu.VMEM((128, 128), jnp.int32), pltpu.VMEM((groups * 8, 256), F32)],
+            compiler_params=pltpu.CompilerParams(vmem_limit_bytes=VMEM_LIMIT),
+            name="node_sums",
+        )(sums, injected, connectivity, disp_start, veloc_start, mass_rows)
 
     return run
 

time: 93 us -> 85.8 us (0.923)
  Pallas kernels: 89 us -> 85 us
  local copies, waits for them, and re-layouts: 3.2 us -> 0 us
    pallas_call x1, Pallas kernels: 89 us -> 76.7 us  [run(): pl.pallas_call(lambda *refs: mega_kernel(n_slab, n_sec, *refs), out_shape...]
    pallas_call x0 -> x1, Pallas kernels: none -> 8.26 us  [run(): pl.pallas_call(collect_kernel, out_shape=(jax.ShapeDtypeStruct((3, nodes)...]
    unnamed x2 -> x0, local copies, waits for them, and re-layouts: 3.2 us -> none
where the time goes in v3:
time: 85.8 us; the launch traced here: 85.6 us
  Pallas kernels  85 us (99%)
    pallas_call x1, Pallas kernels, run(): pl.pallas_call(lambda *refs: mega_kernel(n_slab, n_sec, *refs), out_shape...  76.7 us
    pallas_call x1, Pallas kernels, run(): pl.pallas_call(collect_kernel, out_shape=(jax.ShapeDtypeStruct((3, nodes)...  8.26 us

profile of v3, /device:TPU:1, one launch (start us, length us, event | category | flops | bytes accessed | tf_op | source)
XLA Modules:
  0.0 85.6 jit_solution(7416175503942249491)
XLA Ops:
  0.6 76.7 %slab_window.1 = (f32[1024,128]{1,0:T(8,128)}, f32[2,480,128]{2,1,0:T(8,128)}) custom-call(f32[17,12,1152]{2,1,0:T(8,128)} %refs_0_.1, f32[8,1152]{1,0:T(8,128)} %refs_1_.1, s32[12,1,128]{2,1,0:T(1,128)} %bitcast.15, s32[64,128]{1,0:T(8,128)} %bitcast.13, s32[64,128]{1,0:T(8,128)} %bitcast.14, f32[3,9600]{1,0:T(4,128)} %disp_ref.1, f32[3,9600]{1,0:T(4,128)} %veloc_ref.1, ...), custom_call_target="tpu_custom_call" | custom-call | tf_op jit(solution)/shard_map/slab_window/pallas_call | solution.py:707
  77.4 8.3 %node_sums.1 = (f32[3,9600]{1,0:T(4,128)}, f32[3,9600]{1,0:T(4,128)}) custom-call(f32[1024,128]{1,0:T(8,128)} %get-tuple-element.4.acc_s, f32[2,480,128]{2,1,0:T(8,128)} %get-tuple-element.5.dep_s, s32[125,128]{1,0:T(8,128)} %conn_ref.1, f32[3,9600]{1,0:T(4,128)} %disp_ref.1, f32[3,9600]{1,0:T(4,128)} %veloc_ref.1, f32[75,128]{1,0:T(8,128)} %bitcast.12), custom_call_target="tpu_custom_call" | custom-call | tf_op jit(solution)/shard_map/node_sums/pallas_call | solution.py:780

commit v4 on v3

--- a/solution.py
+++ b/solution.py
@@ -253,7 +253,7 @@
     corners = [(x, y) for x in (prv_x, nxt_x) for y in (prv_y, nxt_y)]
 
     def place(d):
-        return (d // n_sec, lax.rem(d, n_sec))
+        return (lax.div(d, n_sec), lax.rem(d, n_sec))
 
     barrier = pltpu.get_barrier_semaphore()
 
@@ -478,7 +478,7 @@
             send_points(4 * g + q + 64)
         return carry
 
-    lax.fori_loop(0, 16, pick_points, 0, unroll=2)
+    lax.fori_loop(0, 16, pick_points, 0, unroll=4)
     for copy in dcopies:
         copy.wait()
     for a in range(2):
@@ -524,7 +524,7 @@
         dep_s[1] += res[:, 128:256]
         return carry
 
-    lax.fori_loop(0, 16, deposit, 0, unroll=4)
+    lax.fori_loop(0, 16, deposit, 0, unroll=8)
 
     for n in range(4):
         sides = []
@@ -639,27 +639,30 @@
     groups = -(-nodes // 256)
     conn_s[...] = jnp.full(conn_s.shape, 1 << 20, jnp.int32)
     conn_s[0:125, :] = conn_ref[...]
+    blocks = -(-groups // 8)
 
     val_s[...] = jnp.zeros(val_s.shape, F32)
-    sub8 = lax.broadcasted_iota(jnp.int32, (16, 512), 0) // 8
+    sub6 = lax.broadcasted_iota(jnp.int32, (48, 512), 0) // 6
 
     def collect(g, carry):
         idx = lanes_of_rows(conn_s, 4 * g, 4)
         vals = []
         for q in range(4):
             six = acc_s[pl.ds(4 * g + q, 8, stride=128), :]
-            vals.append(jnp.concatenate([six, six], axis=0))
-        vhi, vlo = split2(jnp.concatenate(vals, axis=1))
+            vals.append(six[0:6])
+        val = jnp.concatenate(vals, axis=1)
+        val = jnp.concatenate([val] * 4, axis=0)
+        vhi, vlo = split2(jnp.concatenate([val, val], axis=0))
         oh = one_hot(jnp.bitwise_and(idx, 255), 512)
         high = jnp.minimum(lax.shift_right_logical(idx, 8), 200)
-        hb = (jnp.broadcast_to(high, (16, 512)) - sub8).astype(F32).astype(BF16)
-        zero = jnp.zeros((16, 512), BF16)
-        masks = [hb == jnp.asarray(2 * q, BF16) for q in range(groups // 2)]
+        hb = (jnp.broadcast_to(high, (48, 512)) - sub6).astype(F32).astype(BF16)
+        zero = jnp.zeros((48, 512), BF16)
+        masks = [hb == jnp.asarray(8 * q, BF16) for q in range(blocks)]
         lhs = [jnp.where(mask, v, zero) for v in (vhi, vlo) for mask in masks]
         res = lax.dot_general(
             jnp.concatenate(lhs, axis=0), oh, (((1,), (1,)), ((), ())), preferred_element_type=F32
         )
-        val_s[...] += res[0 : groups * 8] + res[groups * 8 : groups * 16]
+        val_s[...] += res[0 : blocks * 48] + res[blocks * 48 : blocks * 96]
         return carry
 
     lax.fori_loop(0, 32, collect, 0, unroll=8)
@@ -670,8 +673,8 @@
         big = h // 2
         inv = DT / mass_ref[h : h + 1, :]
         inj = [dep_s[h % 2, 12 * big + 3 * n : 12 * big + 3 * n + 3, :] for n in range(4)]
-        vsum = inj[0] + inj[1] + inj[2] + inj[3] + val_s[8 * big : 8 * big + 3, lanes]
-        usum = 4.0 * inj[0] + 3.0 * inj[1] + 2.0 * inj[2] + inj[3] + val_s[8 * big + 3 : 8 * big + 6, lanes]
+        vsum = inj[0] + inj[1] + inj[2] + inj[3] + val_s[6 * big : 6 * big + 3, lanes]
+        usum = 4.0 * inj[0] + 3.0 * inj[1] + 2.0 * inj[2] + inj[3] + val_s[6 * big + 3 : 6 * big + 6, lanes]
         v0 = veloc_ref[:, at]
         outv_ref[:, at] = v0 + inv * vsum
         outd_ref[:, at] = disp_ref[:, at] + (4.0 * DT) * v0 + (DT * inv) * usum
@@ -785,7 +788,7 @@
             ),
             in_specs=[vmem] * 6,
             out_specs=(vmem, vmem),
-            scratch_shapes=[pltpu.VMEM((128, 128), jnp.int32), pltpu.VMEM((groups * 8, 256), F32)],
+            scratch_shapes=[pltpu.VMEM((128, 128), jnp.int32), pltpu.VMEM((-(-groups // 8) * 48, 256), F32)],
             compiler_params=pltpu.CompilerParams(vmem_limit_bytes=VMEM_LIMIT),
             name="node_sums",
         )(sums, injected, connectivity, disp_start, veloc_start, mass_rows)

time: 85.8 us -> 83.4 us (0.972)
  Pallas kernels: 85 us -> 82.6 us
    pallas_call x1, Pallas kernels: 76.7 us -> 75.4 us  [run(): pl.pallas_call(lambda *refs: mega_kernel(n_slab, n_sec, *refs), out_shape...]
    pallas_call x1, Pallas kernels: 8.26 us -> 7.2 us  [run(): pl.pallas_call(collect_kernel, out_shape=(jax.ShapeDtypeStruct((3, nodes)...]
where the time goes in v4:
time: 83.4 us; the launch traced here: 83.2 us
  Pallas kernels  82.6 us (99%)
    pallas_call x1, Pallas kernels, run(): pl.pallas_call(lambda *refs: mega_kernel(n_slab, n_sec, *refs), out_shape...  75.4 us
    pallas_call x1, Pallas kernels, run(): pl.pallas_call(collect_kernel, out_shape=(jax.ShapeDtypeStruct((3, nodes)...  7.2 us

profile of v4, /device:TPU:1, one launch (start us, length us, event | category | flops | bytes accessed | tf_op | source)
XLA Modules:
  0.0 83.2 jit_solution(2283649295136253909)
XLA Ops:
  0.6 75.4 %slab_window.1 = (f32[1024,128]{1,0:T(8,128)}, f32[2,480,128]{2,1,0:T(8,128)}) custom-call(f32[17,12,1152]{2,1,0:T(8,128)} %refs_0_.1, f32[8,1152]{1,0:T(8,128)} %refs_1_.1, s32[12,1,128]{2,1,0:T(1,128)} %bitcast.15, s32[64,128]{1,0:T(8,128)} %bitcast.13, s32[64,128]{1,0:T(8,128)} %bitcast.14, f32[3,9600]{1,0:T(4,128)} %disp_ref.1, f32[3,9600]{1,0:T(4,128)} %veloc_ref.1, ...), custom_call_target="tpu_custom_call" | custom-call | tf_op jit(solution)/shard_map/slab_window/pallas_call | solution.py:710
  76.0 7.2 %node_sums.1 = (f32[3,9600]{1,0:T(4,128)}, f32[3,9600]{1,0:T(4,128)}) custom-call(f32[1024,128]{1,0:T(8,128)} %get-tuple-element.4.acc_s, f32[2,480,128]{2,1,0:T(8,128)} %get-tuple-element.5.dep_s, s32[125,128]{1,0:T(8,128)} %conn_ref.1, f32[3,9600]{1,0:T(4,128)} %disp_ref.1, f32[3,9600]{1,0:T(4,128)} %veloc_ref.1, f32[75,128]{1,0:T(8,128)} %bitcast.12), custom_call_target="tpu_custom_call" | custom-call | tf_op jit(solution)/shard_map/node_sums/pallas_call | solution.py:783
